TPU v7x, 32 devices: a whole 2x2x4 slice. The times are simulated.
32 devices in a mesh: groups: 2 (over y), row: 4 (over z), col: 2 (over x), depth: 2 (over core).
Axes of the slice: x: 2, y: 2, z: 4, core: 2. Of those that a mesh axis runs over, the one named last changes fastest.
Arguments:
- density: float32 [512, 4096], P(('groups', 'row', 'col', 'depth')), parts along dimension 0, may hold values from -0.8 to 0.8
- square_left: int32 [32768], P(('groups', 'row', 'col', 'depth')), parts along dimension 0, may hold values from 0 to 63
- square_right: int32 [32768], P(('groups', 'row', 'col', 'depth')), parts along dimension 0, may hold values from 0 to 63
- square_out: int32 [32768], P(('groups', 'row', 'col', 'depth')), parts along dimension 0, may hold values from 0 to 31
- square_count: int32 [32], P(('groups', 'row', 'col', 'depth')), parts along dimension 0, may hold values from 128 to 1024, as said below
- cube_left: int32 [32768], P(('groups', 'row', 'col', 'depth')), parts along dimension 0, may hold values from 0 to 63
- cube_right: int32 [32768], P(('groups', 'row', 'col', 'depth')), parts along dimension 0, may hold values from 0 to 63
- cube_out: int32 [32768], P(('groups', 'row', 'col', 'depth')), parts along dimension 0, may hold values from 0 to 31
- cube_count: int32 [32], P(('groups', 'row', 'col', 'depth')), parts along dimension 0, may hold values from 128 to 1024, as said below
Outputs:
- purified: float32 [512, 4096], P(('groups', 'row', 'col', 'depth')), parts along dimension 0
There are 2 independent parts, one for each index of `groups`. A program takes and returns all parts, laid end to end along the dimension named above; each array names one. Nothing has to cross between parts.
Inputs may be any that keep to these rules, and one draw needn't show every extreme that they name: `square_count`: each device has an eighth, a quarter, a half or all of 1024 live tasks, and some device of every copy has all 1024. `cube_count`: as for square_count.
All inputs are finite; a program needn't handle non-finite values.
Results may differ from a plain program's by a relative error of at most 0.0003.
Values sent between devices are 32-bit elements; how exact they have to be, the bound alone decides.
No kernel may reach another device: no remote copies, remote signals or barrier semaphores. Data moves between devices by JAX's collectives and lax.ppermute only.
A program may use at most 64 MiB of HBM per device.

v0:
```python
import functools
import math

import jax
import jax.numpy as jnp
from jax import lax
from jax.experimental import pallas as pl
from jax.experimental.pallas import tpu as pltpu
from jax.sharding import PartitionSpec as P

OUT_DEV = 16
CHUNK = 8
TURN = 8


def ring(value, axis, step=1):
    size = lax.axis_size(axis)
    return lax.ppermute(value, axis, [(i, (i + step) % size) for i in range(size)])


def ring_all(value, axis):
    pieces = [value]
    for _ in range(lax.axis_size(axis) - 1):
        pieces.append(ring(pieces[-1], axis))
    return pieces


def plan(key, left, out, groups, seg_groups, slots, chunks):
    tasks = key.shape[0]
    place = jnp.arange(tasks, dtype=jnp.int32)
    group = jnp.arange(groups, dtype=jnp.int32)
    segs = groups // seg_groups
    same = (key[:, None] == key[None, :]) & (place[:, None] < place[None, :])
    rank = jnp.sum(same.astype(jnp.int32), axis=0)
    count = jnp.sum((key[:, None] == group[None, :]).astype(jnp.int32), axis=0)
    filled = (count + CHUNK - 1) // CHUNK
    seg_id = group // seg_groups
    earlier = (group[:, None] < group[None, :]) & (seg_id[:, None] == seg_id[None, :])
    within = jnp.sum(jnp.where(earlier, filled[:, None], 0), axis=0)
    total = jnp.sum(filled.reshape(segs, seg_groups), axis=1)
    turns = (total + TURN - 1) // TURN
    seg = jnp.arange(segs, dtype=jnp.int32)
    first = jnp.sum(jnp.where(seg[:, None] < seg[None, :], turns[:, None], 0), axis=0)
    base = within + TURN * jnp.sum(
        jnp.where(seg_id[:, None] == seg[None, :], first[None, :], 0), axis=1
    )
    start = jnp.sum(jnp.where(key[:, None] == group[None, :], base[None, :] * CHUNK, 0), axis=1)
    position = jnp.where(key < groups, start + rank, -1)
    slot = jnp.arange(chunks * CHUNK, dtype=jnp.int32)
    code = jnp.sum(
        jnp.where(
            position[:, None] == slot[None, :], (left * (slots + 1) + out - slots)[:, None], 0
        ),
        axis=0,
    ) + slots
    chunk = jnp.arange(chunks, dtype=jnp.int32)
    rights = jnp.sum((base + filled)[:, None] <= chunk[None, :], axis=0, dtype=jnp.int32)
    return dict(
        first=first,
        turns=turns,
        rights=rights,
        left=code // (slots + 1) * 64,
        out=code % (slots + 1) * 64,
    )


def spread(source, flat):
    for high in range(0, source.shape[0], 8):
        for pair in range(32):
            flat[pl.ds(high * 32 + pair, 8, stride=32), :] = source[
                high : high + 8, pair * 128 : pair * 128 + 128
            ]


def low_half(rows):
    return lax.broadcasted_iota(jnp.int32, (rows, 128), 1) < 64


def split(value):
    top = value.astype(jnp.bfloat16).astype(jnp.float32)
    return top, value - top


def fill_panel(sources, panel, first, flat):
    low = low_half(32)
    for index, source in enumerate(sources):
        spread(source, flat)
        for block in range(16):
            row = (first + index) * 1024 + block * 64
            top, rest = split(flat[block * 32 : block * 32 + 32, :])
            even = jnp.where(low, top, pltpu.roll(rest, 64, 1))
            odd = jnp.where(low, pltpu.roll(top, 64, 1), rest)
            panel[pl.ds(row, 32), :] = even.astype(jnp.bfloat16)
            panel[pl.ds(row + 32, 32), :] = odd.astype(jnp.bfloat16)


def fill_weights(sources, weights, flat, tall):
    low, low_tall = low_half(32), low_half(64)
    for index, source in enumerate(sources):
        spread(source, flat)
        for block in range(16):
            both = flat[block * 32 : block * 32 + 32, :]
            swapped = pltpu.roll(both, 64, 1)
            spot = block % 4 * 64
            tall[pl.ds(spot, 32, stride=2), :] = jnp.where(low, both, swapped)
            tall[pl.ds(spot + 1, 32, stride=2), :] = jnp.where(low, swapped, both)
            top, rest = split(tall[spot : spot + 64, :])
            weights[index * 16 + block, 0:64] = jnp.where(low_tall, top, rest).astype(jnp.bfloat16)
            weights[index * 16 + block, 64:128] = jnp.where(low_tall, top, 0.0).astype(jnp.bfloat16)


def prepare_kernel(raw_lefts, *refs):
    sources, (panel, weights, flat, tall) = refs[:-4], refs[-4:]
    fill_panel(sources[:raw_lefts], panel, 0, flat)
    fill_weights(sources[raw_lefts:], weights, flat, tall)


def prepare(lefts, rights):
    vmem = pl.BlockSpec(memory_space=pltpu.VMEM)
    return pl.pallas_call(
        functools.partial(prepare_kernel, len(lefts)),
        out_shape=[
            jax.ShapeDtypeStruct((len(lefts) * 1024, 128), jnp.bfloat16),
            jax.ShapeDtypeStruct((len(rights) * 16, 128, 128), jnp.bfloat16),
        ],
        in_specs=[vmem] * (len(lefts) + len(rights)),
        out_specs=[vmem] * 2,
        scratch_shapes=[pltpu.VMEM((size, 128), jnp.float32) for size in (512, 256)],
        compiler_params=pltpu.CompilerParams(vmem_limit_bytes=44 << 20),
    )(*lefts, *rights)


def kernel(raw_lefts, raw_rights, has_left, has_right, has_sum, last, slots, first_group, segs, keep, refs):
    refs = list(refs)
    first, turn_count, rights, lefts, outs = refs[:5]
    refs = refs[5:]
    left_raw, refs = refs[:raw_lefts], refs[raw_lefts:]
    right_raw, refs = refs[:raw_rights], refs[raw_rights:]
    panel, given, sum_in = None, [], None
    if has_left:
        panel, refs = refs[0], refs[1:]
    given, refs = refs[:has_right], refs[has_right:]
    if has_sum:
        sum_in, refs = refs[0], refs[1:]
    results, refs = refs[:2] if last else refs[:1], refs[2:] if last else refs[1:]
    flat, tall, folded, sum_0, sum_1 = refs[-5:]
    start = 0
    if raw_lefts:
        whole, refs = refs[0], refs[1:]
        if has_left:
            start = panel.shape[0] // 1024
            whole[: panel.shape[0], :] = panel[...]
        panel = whole
    weights = refs[0] if raw_rights else given[0]
    sums = (sum_0, sum_1)
    fill_panel(left_raw, panel, start, flat)
    fill_weights(right_raw, weights, flat, tall)

    sum_1[...] = jnp.zeros_like(sum_1)
    if has_sum:
        sum_0[...] = sum_in[...]
    else:
        sum_0[...] = jnp.zeros_like(sum_0)

    zero = jnp.zeros((128, 128), jnp.bfloat16)
    limit = weights.shape[0] - 1
    most = panel.shape[0] - 64

    def issue(chunk, unit, totals):
        first_right, second_right = (
            weights[jnp.clip(rights[chunk + side] - first_group, 0, limit)] for side in range(2)
        )
        pltpu.matmul_push_rhs(
            jnp.concatenate(
                [
                    jnp.concatenate([first_right, zero], 1),
                    jnp.concatenate([zero, second_right], 1),
                ],
                0,
            ),
            0,
            unit,
        )
        for task, total in enumerate(totals):
            sides = []
            for side in range(2):
                row = jnp.minimum(lefts[(chunk + side) * CHUNK + task], most)
                sides.append(panel[pl.ds(pl.multiple_of(row, 64), 64), :])
            pltpu.matmul_acc_lhs(
                total, jnp.concatenate(sides, 1), load_staged_rhs=0 if task == 0 else None
            )

    def drain(chunk, unit, totals):
        for task, total in enumerate(totals):
            product = pltpu.matmul_pop(total)
            for side in range(2):
                row = outs[(chunk + side) * CHUNK + task]
                rows = pl.ds(pl.multiple_of(row, 64), 64)
                sums[unit][rows, :] += product[:, side * 128 : side * 128 + 128]

    def work(*totals):
        totals = [totals[index : index + CHUNK] for index in range(0, len(totals), CHUNK)]
        begin, turns = first[segs[0]] * TURN, turn_count[segs[0]]
        for seg in segs[1:]:
            turns = turns + turn_count[seg]
        for unit in range(2):
            issue(begin + 2 * unit, unit, totals[unit])

        @pl.loop(0, turns)
        def _(turn):
            chunk = begin + turn * TURN
            for unit in range(2):
                issue(chunk + 4 + 2 * unit, unit, totals[2 + unit])
            for unit in range(2):
                drain(chunk + 2 * unit, unit, totals[unit])
            for unit in range(2):
                issue(chunk + 8 + 2 * unit, unit, totals[unit])
            for unit in range(2):
                drain(chunk + 4 + 2 * unit, unit, totals[2 + unit])

        for unit in range(2):
            for total in totals[unit]:
                pltpu.matmul_pop(total)

    pl.run_scoped(
        work,
        *[
            pltpu.ACC(unit)((64, 256), jnp.float32)
            for _ in range(2)
            for unit in range(2)
            for _ in range(CHUNK)
        ],
    )

    if not last:
        results[0][...] = sum_0[...] + sum_1[...]
        return
    low = low_half(32)
    for block in range(slots):
        rows = pl.ds(block * 64, 64)
        value = sum_0[rows, :] + sum_1[rows, :]
        value = value + pltpu.roll(value, 64, 1)
        folded[pl.ds(block * 32, 32), :] = jnp.where(low, value[:32], value[32:])
    layer = lax.axis_index("depth")
    size = results[0].shape[0]
    layers = slots // size
    for index, result in enumerate(results):
        row = (layer * size if index == 0 else lax.rem(layer + 1, layers) * size) * 32
        for high in range(0, size, 8):
            for pair in range(32):
                result[high : high + 8, pair * 128 : pair * 128 + 128] = folded[
                    pl.ds(row + high * 32 + pair, 8, stride=32), :
                ]


def tile_sum(tasks, seg, seg_count, left_raw, right_raw, panel, given, sum_in, last, slots, width, first_group, keep=False):
    f32, bf16 = jnp.float32, jnp.bfloat16
    plans = [tasks[name] for name in ("first", "turns", "rights", "left", "out")]
    args = [*plans, *left_raw, *right_raw]
    smem, vmem = pl.BlockSpec(memory_space=pltpu.SMEM), pl.BlockSpec(memory_space=pltpu.VMEM)
    extra = [v for v in [panel, *given, sum_in] if v is not None]
    in_specs = [smem] * 5 + [vmem] * (len(left_raw) + len(right_raw) + len(extra))
    sum_shape = ((slots + 1) * 64, 128)
    shapes = (
        [jax.ShapeDtypeStruct((OUT_DEV, width), f32)] * 2
        if last
        else [jax.ShapeDtypeStruct(sum_shape, f32)]
    )
    blocks = len(left_raw) * 1024 + (0 if panel is None else panel.shape[0])
    scratch = []
    if left_raw and keep:
        shapes.append(jax.ShapeDtypeStruct((blocks, 128), bf16))
    elif left_raw:
        scratch = [pltpu.VMEM((blocks, 128), bf16)]
    if right_raw:
        shapes.append(jax.ShapeDtypeStruct((len(right_raw) * 16, 128, 128), bf16))
    body = functools.partial(
        kernel,
        len(left_raw),
        len(right_raw),
        panel is not None,
        len(given),
        sum_in is not None,
        last,
        slots,
        first_group,
        tuple(range(seg, seg + seg_count)),
        keep,
    )
    return pl.pallas_call(
        lambda *refs: body(refs),
        out_shape=shapes,
        in_specs=in_specs,
        out_specs=[vmem] * len(shapes),
        scratch_shapes=[
            *scratch,
            pltpu.VMEM((512, 128), f32),
            pltpu.VMEM((256, 128), f32),
            pltpu.VMEM((slots * 32 if last else 8, 128), f32),
            pltpu.VMEM(sum_shape, f32),
            pltpu.VMEM(sum_shape, f32),
        ],
        compiler_params=pltpu.CompilerParams(vmem_limit_bytes=44 << 20),
    )(*args, *extra)


def local(
    density,
    square_left,
    square_right,
    square_out,
    square_count,
    cube_left,
    cube_right,
    cube_out,
    cube_count,
):
    per_dev, width = density.shape
    rows, cols, layers = (lax.axis_size(name) for name in ("row", "col", "depth"))
    row, col, layer = (lax.axis_index(name) for name in ("row", "col", "depth"))
    slots = layers * OUT_DEV
    tasks = square_left.shape[0]
    place = jnp.arange(tasks, dtype=jnp.int32)

    def moved_left(left):
        from_col = lax.rem(col - left // (layers * per_dev) + cols, cols)
        from_layer = lax.rem(layer - left // per_dev % layers + layers, layers)
        return from_col, (from_col * layers + from_layer) * per_dev + left % per_dev

    def moved_right(right):
        away = lax.rem(row - right // per_dev + rows, rows)
        order = jnp.where(
            2 * away <= rows - 1 + rows % 2, 2 * away - 1, jnp.minimum(2 * (rows - away), rows - 1)
        )
        return jnp.maximum(order, 0) * per_dev + right % per_dev

    column = [density]
    for _ in range((rows - 1) // 2):
        ahead, behind = (column[-2], column[-1]) if len(column) > 1 else (density, density)
        column += [ring(ahead, "row"), ring(behind, "row", -1)]
    across = ring_all(density, "col")
    lefts = [piece for value in across for piece in ring_all(value, "depth")]

    groups = rows * per_dev
    _, left = moved_left(square_left)
    key = jnp.where(place < square_count[0], moved_right(square_right), groups)
    chunks = -(-(tasks // CHUNK + groups + TURN * rows + TURN) // 16) * 16
    square_tasks = plan(key, left, square_out, groups, per_dev, slots, chunks)
    from_col, left = moved_left(cube_left)
    left = left - jnp.where(from_col == 0, 0, layers * per_dev)
    key = jnp.where(from_col == 0, 0, groups) + moved_right(cube_right)
    key = jnp.where(place < cube_count[0], key, 2 * groups)
    chunks = -(-(tasks // CHUNK + 2 * groups + TURN * 2 + TURN) // 16) * 16
    cube_tasks = plan(key, left, cube_out, 2 * groups, groups, slots, chunks)

    panel, first = prepare(lefts[:layers], column[:1])
    total, panel = tile_sum(
        square_tasks, 0, 1, lefts[layers:], [], panel, [first], None, False, slots, width, 0, True
    )
    weights = [first]
    if rows % 2 == 0:
        column[-2], total = lax.optimization_barrier((column[-2], total))
        opposite = ring(column[-2] if rows > 2 else density, "row")
    for seg in range(1, len(column), 2):
        last = rows % 2 == 1 and seg + 2 == rows
        *result, piece = tile_sum(
            square_tasks, seg, 2, [], column[seg : seg + 2], panel, [], total, last,
            slots, width, seg * per_dev,
        )
        total = result[0]
        weights.append(piece)
    if rows % 2 == 0:
        *result, piece = tile_sum(
            square_tasks, rows - 1, 1, [], [opposite], panel, [], total, True,
            slots, width, (rows - 1) * per_dev,
        )
        weights.append(piece)
    mine, other = result
    weights = jnp.concatenate(weights, axis=0)
    square = mine + ring(other, "depth")

    near = ring_all(square, "depth")
    far = ring_all(square, "col")[1:]
    (total,) = tile_sum(
        cube_tasks, 0, 1, near, [], None, [weights], None, False, slots, width, 0
    )
    total, *far = lax.optimization_barrier((total, *far))
    far = [piece for value in far for piece in ring_all(value, "depth")]
    mine, other = tile_sum(
        cube_tasks, 1, 1, far, [], None, [weights], total, True, slots, width, groups
    )
    cube = mine + ring(other, "depth")
    return 3.0 * square - 2.0 * cube


def solution(mesh):
    return jax.shard_map(
        local,
        mesh=mesh,
        in_specs=(
            P(("groups", "row", "col", "depth"), None),
            P(("groups", "row", "col", "depth")),
            P(("groups", "row", "col", "depth")),
            P(("groups", "row", "col", "depth")),
            P(("groups", "row", "col", "depth")),
            P(("groups", "row", "col", "depth")),
            P(("groups", "row", "col", "depth")),
            P(("groups", "row", "col", "depth")),
            P(("groups", "row", "col", "depth")),
        ),
        out_specs=P(("groups", "row", "col", "depth"), None),
        check_vma=False,
    )
```

profile of v0, /device:TPU:5, one launch (start us, length us, event | category | flops | bytes accessed | tf_op | source)
XLA Modules:
  0.0 53.0 jit_solution(6602145827763999327)
XLA Ops:
  0.0 1.3 %collective-permute-start = (f32[16,4096]{1,0:T(8,128)}, f32[16,4096]{1,0:T(8,128)S(1)}, u32[]{:S(2)}, u32[]{:S(2)}) collective-permute-start(f32[16,4096]{1,0:T(8,128)} %refs_2_.1), channel_id=1, source_target_pairs={{0,4},{4,8},{8,12},{12,0},{1,5},{5,9},{9,13},{13,1},{2,6},{6,10},{... | collective-permute-start | bytes 786440 | tf_op jit(solution)/shard_map/ppermute | solution.py:18
  1.3 1.2 %collective-permute-start.1 = (f32[16,4096]{1,0:T(8,128)}, f32[16,4096]{1,0:T(8,128)S(1)}, u32[]{:S(2)}, u32[]{:S(2)}) collective-permute-start(f32[16,4096]{1,0:T(8,128)} %refs_2_.1), channel_id=1, source_target_pairs={{0,2},{2,0},{1,3},{3,1},{4,6},{6,4},{5,7},{7,5},{8,10},{10,8},{9,1... | collective-permute-start | bytes 786440 | tf_op jit(solution)/shard_map/ppermute | solution.py:18
  2.5 1.2 %collective-permute-start.3 = (f32[16,4096]{1,0:T(8,128)}, f32[16,4096]{1,0:T(8,128)S(1)}, u32[]{:S(2)}, u32[]{:S(2)}) collective-permute-start(f32[16,4096]{1,0:T(8,128)} %refs_2_.1), channel_id=1, source_target_pairs={{0,1},{1,0},{2,3},{3,2},{4,5},{5,4},{6,7},{7,6},{8,9},{9,8},{10,11... | collective-permute-start | bytes 786440 | tf_op jit(solution)/shard_map/ppermute | solution.py:18
  3.7 2.0 %collective-permute-start.5 = (f32[16,4096]{1,0:T(8,128)}, f32[16,4096]{1,0:T(8,128)S(1)}, u32[]{:S(2)}, u32[]{:S(2)}) collective-permute-start(f32[16,4096]{1,0:T(8,128)} %refs_2_.1), channel_id=1, source_target_pairs={{0,12},{4,0},{8,4},{12,8},{1,13},{5,1},{9,5},{13,9},{2,14},{6,2},{... | collective-permute-start | bytes 786440 | tf_op jit(solution)/shard_map/ppermute | solution.py:18
  6.4 0.8 %fusion.49 = (s32[1024]{0:T(1024)S(1)}, s32[1024]{0:T(1024)S(1)}, s32[1024]{0:T(1024)S(1)}) fusion(s32[1024]{0:T(1024)} %param.16, s32[1024]{0:T(1024)} %param.14, s32[]{:T(128)S(6)} %axis_index.38, s32[]{:T(128)S(6)} %axis_index.36, s32[1024]{0:T(1024)} %param.15, s32[]{:T(128)S(6)} %axis_index.33, s32[]{:T(128)} %bitcast.4, s32[1024]{0:T(1024)} %param.12, ...), kind=kLoop, calls=%fused_computation.126 | loop fusion | flops 174080 | bytes 32784 | tf_op jit(solution)/shard_map/sub | solution.py:52
  7.2 0.2 convert_reduce_fusion.2
  7.4 0.4 convert_reduce_fusion
  8.5 0.7 %fusion.14 = s32[1024]{0:T(1024)S(1)} fusion(s32[1024]{0:T(1024)} %param.11, s32[]{:T(128)S(6)} %axis_index.33, s32[]{:T(128)} %bitcast.2), kind=kLoop, calls=%fused_computation.91 | loop fusion | flops 39936 | bytes 8200 | tf_op jit(solution)/shard_map/jit(_where)/select_n | solution.py:346
  9.2 0.1 convert_reduce_fusion.3
  9.3 0.4 convert_reduce_fusion.1
  9.7 0.1 sub.189
  9.8 0.1 fusion.61
  10.0 0.1 fusion.59.refs_0_
  10.0 0.1 select_reduce_fusion.4
  10.2 0.1 fusion.60
  10.2 0.1 sub.165
  10.3 0.1 fusion.57
  10.5 0.1 select_reduce_fusion.7.refs_0_
  10.6 0.1 select_reduce_fusion.5
  10.7 0.1 select_reduce_fusion.6
  10.8 0.1 select_reduce_fusion.3
  10.9 0.7 %add_select_fusion.17 = s32[1024]{0:T(1024)S(1)} fusion(s32[1024]{0:T(1024)S(1)} %select_reduce_fusion.3, s32[1024]{0:T(1024)S(1)} %convert_reduce_fusion.1, s32[1024]{0:T(1024)} %param.11, s32[]{:T(128)S(6)} %axis_index.33, s32[]{:T(128)} %bitcast.3), kind=kLoop, calls=%fused_computation.132 | loop fusion | flops 43008 | bytes 16392 | tf_op jit(solution)/shard_map/jit(_where)/select_n | solution.py:48
  11.6 1.0 %select_reduce_fusion.1 = s32[1920]{0:T(1024)S(1)} fusion(s32[1024]{0:T(1024)S(1)} %get-tuple-element.49, s32[1024]{0:T(1024)S(1)} %add_select_fusion.17), kind=kLoop, calls=%fused_computation.2 | loop fusion | flops 5896320 | bytes 15872 | tf_op jit(solution)/shard_map/reduce_sum | solution.py:50
  12.7 0.4 select_reduce_fusion.2
  13.0 0.0 collective-permute-done.1.refs_5_
  13.0 0.3 collective-permute-start.2
  13.4 0.1 convert_reduce_fusion.5.refs_2_
  13.5 0.0 collective-permute-done.3.refs_1_
  13.5 0.0 copy-start
  13.5 0.9 %copy-done = f32[16,4096]{1,0:T(8,128)S(1)} copy-done((f32[16,4096]{1,0:T(8,128)S(1)}, f32[16,4096]{1,0:T(8,128)}, u32[]{:S(2)}) %copy-start) | copy-done | bytes 262168
  14.5 0.8 %shard_map.91 = (bf16[2048,128]{1,0:T(8,128)(2,1)S(1)}, bf16[16,128,128]{2,1,0:T(8,128)(2,1)S(1)}) custom-call(f32[16,4096]{1,0:T(8,128)S(1)} %copy-done, f32[16,4096]{1,0:T(8,128)S(1)} %collective-permute-done.3.refs_1_, f32[16,4096]{1,0:T(8,128)S(1)} %copy-done), custom_call_target="tpu_custom_call" | custom-call | tf_op jit(solution)/shard_map/pallas_call | solution.py:120
  15.2 0.0 collective-permute-done.2.refs_6_
  15.3 2.9 %shard_map.92 = (f32[2112,128]{1,0:T(8,128)S(1)}, bf16[4096,128]{1,0:T(8,128)(2,1)S(1)}) custom-call(s32[4]{0:T(128)S(1)} %select_reduce_fusion.7.refs_0_, s32[4]{0:T(128)S(1)} %and_select_fusion.6.refs_1_, s32[240]{0:T(256)S(1)} %convert_reduce_fusion.5.refs_2_, s32[1920]{0:T(1024)S(1)} %get-tuple-element.38.refs_3_, s32[1920]{0:T(1024)S(1)} %get-tuple-element.37.refs_4_, ...), custom_call_target="tpu_custom_call" | custom-call | tf_op jit(solution)/shard_map/pallas_call | solution.py:290
  18.1 0.0 collective-permute-done.refs_5_
  18.2 0.1 collective-permute-start.4
  18.2 1.4 %select_reduce_fusion = s32[2304]{0:T(1024)S(1)} fusion(s32[1024]{0:T(1024)S(1)} %get-tuple-element.39, s32[1024]{0:T(1024)S(1)} %add_select_fusion.16), kind=kLoop, calls=%fused_computation | loop fusion | flops 7075584 | bytes 17408 | tf_op jit(solution)/shard_map/reduce_sum | solution.py:50
  19.6 0.0 collective-permute-done.5.refs_6_
  19.6 3.7 %shard_map.93 = (f32[2112,128]{1,0:T(8,128)S(1)}, bf16[32,128,128]{2,1,0:T(8,128)(2,1)S(1)}) custom-call(s32[4]{0:T(128)S(1)} %select_reduce_fusion.7.refs_0_, s32[4]{0:T(128)S(1)} %and_select_fusion.6.refs_1_, s32[240]{0:T(256)S(1)} %convert_reduce_fusion.5.refs_2_, s32[1920]{0:T(1024)S(1)} %get-tuple-element.38.refs_3_, ...), custom_call_target="tpu_custom_call" | custom-call | tf_op jit(solution)/shard_map/pallas_call | solution.py:290
  23.3 4.7 %collective-permute-done.4.refs_5_ = f32[16,4096]{1,0:T(8,128)S(1)} collective-permute-done((f32[16,4096]{1,0:T(8,128)S(1)}, f32[16,4096]{1,0:T(8,128)S(1)}, u32[]{:S(2)}, u32[]{:S(2)}) %collective-permute-start.4) | collective-permute-done | bytes 262176 | tf_op jit(solution)/shard_map/ppermute | solution.py:18
  28.0 3.3 %shard_map.94 = (f32[16,4096]{1,0:T(8,128)S(1)}, f32[16,4096]{1,0:T(8,128)S(1)}, bf16[16,128,128]{2,1,0:T(8,128)(2,1)S(1)}) custom-call(s32[4]{0:T(128)S(1)} %select_reduce_fusion.7.refs_0_, s32[4]{0:T(128)S(1)} %and_select_fusion.6.refs_1_, s32[240]{0:T(256)S(1)} %convert_reduce_fusion.5.refs_2_, s32[1920]{0:T(1024)S(1)} %get-tuple-element.38.refs_3_, ...), custom_call_target="tpu_custom_call" | custom-call | tf_op jit(solution)/shard_map/pallas_call | solution.py:290
  31.3 0.4 collective-permute-start.6
  31.8 0.1 convert_reduce_fusion.4.refs_2_
  32.0 1.0 %collective-permute-done.6 = f32[16,4096]{1,0:T(8,128)S(1)} collective-permute-done((f32[16,4096]{1,0:T(8,128)S(1)}, f32[16,4096]{1,0:T(8,128)S(1)}, u32[]{:S(2)}, u32[]{:S(2)}) %collective-permute-start.6) | collective-permute-done | bytes 262176 | tf_op jit(solution)/shard_map/ppermute | solution.py:18
  33.0 0.4 collective-permute-start.7
  33.4 2.1 %collective-permute-start.8 = (f32[16,4096]{1,0:T(8,128)S(1)}, f32[16,4096]{1,0:T(8,128)S(1)}, u32[]{:S(2)}, u32[]{:S(2)}) collective-permute-start(f32[16,4096]{1,0:T(8,128)S(1)} %add.275.refs_5_), channel_id=1, source_target_pairs={{0,2},{2,0},{1,3},{3,1},{4,6},{6,4},{5,7},{7,5},{8,10},{10,8},{9,1... | collective-permute-start | bytes 786440 | tf_op jit(solution)/shard_map/ppermute | solution.py:18
  35.5 0.2 constant_dynamic-update-slice_fusion.1
  35.6 0.1 constant_dynamic-update-slice_fusion.refs_7_
  35.7 0.0 collective-permute-done.7.refs_6_
  35.7 5.8 %shard_map.95.refs_8_ = f32[2112,128]{1,0:T(8,128)S(1)} custom-call(s32[2]{0:T(128)S(1)} %fusion.59.refs_0_, s32[2]{0:T(128)S(1)} %and_select_fusion.2.refs_1_, s32[288]{0:T(512)S(1)} %convert_reduce_fusion.4.refs_2_, s32[2304]{0:T(1024)S(1)} %get-tuple-element.36.refs_3_, s32[2304]{0:T(1024)S(1)} %get-tuple-element.35.refs_4_, ...), custom_call_target="tpu_custom_call" | custom-call | tf_op jit(solution)/shard_map/pallas_call | solution.py:290
  41.6 0.4 collective-permute-done.8.refs_5_
  42.0 0.7 %collective-permute-start.9 = (f32[16,4096]{1,0:T(8,128)S(1)}, f32[16,4096]{1,0:T(8,128)S(1)}, u32[]{:S(2)}, u32[]{:S(2)}) collective-permute-start(f32[16,4096]{1,0:T(8,128)S(1)} %collective-permute-done.8.refs_5_), channel_id=1, source_target_pairs={{0,1},{1,0},{2,3},{3,2},{4,5},{5,4},{6,7},{7,6},{8,9},{9,8},{10,11... | collective-permute-start | bytes 786440 | tf_op jit(solution)/shard_map/ppermute | solution.py:18
  42.7 1.2 %collective-permute-done.9.refs_6_ = f32[16,4096]{1,0:T(8,128)S(1)} collective-permute-done((f32[16,4096]{1,0:T(8,128)S(1)}, f32[16,4096]{1,0:T(8,128)S(1)}, u32[]{:S(2)}, u32[]{:S(2)}) %collective-permute-start.9) | collective-permute-done | bytes 262176 | tf_op jit(solution)/shard_map/ppermute | solution.py:18
  43.9 6.8 %shard_map.96 = (f32[16,4096]{1,0:T(8,128)S(1)}, f32[16,4096]{1,0:T(8,128)S(1)}) custom-call(s32[2]{0:T(128)S(1)} %fusion.59.refs_0_, s32[2]{0:T(128)S(1)} %and_select_fusion.2.refs_1_, s32[288]{0:T(512)S(1)} %convert_reduce_fusion.4.refs_2_, s32[2304]{0:T(1024)S(1)} %get-tuple-element.36.refs_3_, s32[2304]{0:T(1024)S(1)} %get-tuple-element.35.refs_4_, ...), custom_call_target="tpu_custom_call" | custom-call | tf_op jit(solution)/shard_map/pallas_call | solution.py:290
  50.7 0.1 collective-permute-start.10
  50.8 1.5 %collective-permute-done.10 = f32[16,4096]{1,0:T(8,128)S(1)} collective-permute-done((f32[16,4096]{1,0:T(8,128)S(1)}, f32[16,4096]{1,0:T(8,128)S(1)}, u32[]{:S(2)}, u32[]{:S(2)}) %collective-permute-start.10) | collective-permute-done | bytes 262176 | tf_op jit(solution)/shard_map/ppermute | solution.py:18
  52.3 0.7 %multiply_subtract_fusion = f32[16,4096]{1,0:T(8,128)} fusion(f32[16,4096]{1,0:T(8,128)S(1)} %get-tuple-element.33, f32[16,4096]{1,0:T(8,128)S(1)} %collective-permute-done.10, f32[16,4096]{1,0:T(8,128)S(1)} %add.275.refs_5_), kind=kLoop, calls=%fused_computation.12 | loop fusion | flops 262144 | bytes 1048576 | tf_op jit(solution)/shard_map/sub | solution.py:393
  (12 shorter events, 0.2 us)
Async XLA Ops:
  0.0 18.1 %collective-permute-start = (f32[16,4096]{1,0:T(8,128)}, f32[16,4096]{1,0:T(8,128)S(1)}, u32[]{:S(2)}, u32[]{:S(2)}) collective-permute-start(f32[16,4096]{1,0:T(8,128)} %refs_2_.1), channel_id=1, source_target_pairs={{0,4},{4,8},{8,12},{12,0},{1,5},{5,9},{9,13},{13,1},{2,6},{6,10},{... | collective-permute-start | bytes 786440 | tf_op jit(solution)/shard_map/ppermute | solution.py:18
  1.3 11.7 %collective-permute-start.1 = (f32[16,4096]{1,0:T(8,128)}, f32[16,4096]{1,0:T(8,128)S(1)}, u32[]{:S(2)}, u32[]{:S(2)}) collective-permute-start(f32[16,4096]{1,0:T(8,128)} %refs_2_.1), channel_id=1, source_target_pairs={{0,2},{2,0},{1,3},{3,1},{4,6},{6,4},{5,7},{7,5},{8,10},{10,8},{9,1... | collective-permute-start | bytes 786440 | tf_op jit(solution)/shard_map/ppermute | solution.py:18
  2.5 11.0 %collective-permute-start.3 = (f32[16,4096]{1,0:T(8,128)}, f32[16,4096]{1,0:T(8,128)S(1)}, u32[]{:S(2)}, u32[]{:S(2)}) collective-permute-start(f32[16,4096]{1,0:T(8,128)} %refs_2_.1), channel_id=1, source_target_pairs={{0,1},{1,0},{2,3},{3,2},{4,5},{5,4},{6,7},{7,6},{8,9},{9,8},{10,11... | collective-permute-start | bytes 786440 | tf_op jit(solution)/shard_map/ppermute | solution.py:18
  3.7 15.9 %collective-permute-start.5 = (f32[16,4096]{1,0:T(8,128)}, f32[16,4096]{1,0:T(8,128)S(1)}, u32[]{:S(2)}, u32[]{:S(2)}) collective-permute-start(f32[16,4096]{1,0:T(8,128)} %refs_2_.1), channel_id=1, source_target_pairs={{0,12},{4,0},{8,4},{12,8},{1,13},{5,1},{9,5},{13,9},{2,14},{6,2},{... | collective-permute-start | bytes 786440 | tf_op jit(solution)/shard_map/ppermute | solution.py:18
  13.0 2.2 %collective-permute-start.2 = (f32[16,4096]{1,0:T(8,128)S(1)}, f32[16,4096]{1,0:T(8,128)S(1)}, u32[]{:S(2)}, u32[]{:S(2)}) collective-permute-start(f32[16,4096]{1,0:T(8,128)S(1)} %collective-permute-done.1.refs_5_), channel_id=1, source_target_pairs={{0,1},{1,0},{2,3},{3,2},{4,5},{5,4},{6,7},{7,6},{8,9},{9,8},{10,11... | collective-permute-start | bytes 786440 | tf_op jit(solution)/shard_map/ppermute | solution.py:18
  13.5 1.0 %copy-start = (f32[16,4096]{1,0:T(8,128)S(1)}, f32[16,4096]{1,0:T(8,128)}, u32[]{:S(2)}) copy-start(f32[16,4096]{1,0:T(8,128)} %refs_2_.1) | copy-start | bytes 786436
  18.2 9.9 %collective-permute-start.4 = (f32[16,4096]{1,0:T(8,128)S(1)}, f32[16,4096]{1,0:T(8,128)S(1)}, u32[]{:S(2)}, u32[]{:S(2)}) collective-permute-start(f32[16,4096]{1,0:T(8,128)S(1)} %collective-permute-done.refs_5_), channel_id=1, source_target_pairs={{0,4},{4,8},{8,12},{12,0},{1,5},{5,9},{9,13},{13,1},{2,6},{6,10},{... | collective-permute-start | bytes 786440 | tf_op jit(solution)/shard_map/ppermute | solution.py:18
  31.3 1.6 %collective-permute-start.6 = (f32[16,4096]{1,0:T(8,128)S(1)}, f32[16,4096]{1,0:T(8,128)S(1)}, u32[]{:S(2)}, u32[]{:S(2)}) collective-permute-start(f32[16,4096]{1,0:T(8,128)S(1)} %get-tuple-element.28), channel_id=1, source_target_pairs={{0,1},{1,0},{2,3},{3,2},{4,5},{5,4},{6,7},{7,6},{8,9},{9,8},{10,11... | collective-permute-start | bytes 786440 | tf_op jit(solution)/shard_map/ppermute | solution.py:18
  33.0 2.8 %collective-permute-start.7 = (f32[16,4096]{1,0:T(8,128)S(1)}, f32[16,4096]{1,0:T(8,128)S(1)}, u32[]{:S(2)}, u32[]{:S(2)}) collective-permute-start(f32[16,4096]{1,0:T(8,128)S(1)} %add.275.refs_5_), channel_id=1, source_target_pairs={{0,1},{1,0},{2,3},{3,2},{4,5},{5,4},{6,7},{7,6},{8,9},{9,8},{10,11... | collective-permute-start | bytes 786440 | tf_op jit(solution)/shard_map/ppermute | solution.py:18
  33.4 8.6 %collective-permute-start.8 = (f32[16,4096]{1,0:T(8,128)S(1)}, f32[16,4096]{1,0:T(8,128)S(1)}, u32[]{:S(2)}, u32[]{:S(2)}) collective-permute-start(f32[16,4096]{1,0:T(8,128)S(1)} %add.275.refs_5_), channel_id=1, source_target_pairs={{0,2},{2,0},{1,3},{3,1},{4,6},{6,4},{5,7},{7,5},{8,10},{10,8},{9,1... | collective-permute-start | bytes 786440 | tf_op jit(solution)/shard_map/ppermute | solution.py:18
  42.0 1.9 %collective-permute-start.9 = (f32[16,4096]{1,0:T(8,128)S(1)}, f32[16,4096]{1,0:T(8,128)S(1)}, u32[]{:S(2)}, u32[]{:S(2)}) collective-permute-start(f32[16,4096]{1,0:T(8,128)S(1)} %collective-permute-done.8.refs_5_), channel_id=1, source_target_pairs={{0,1},{1,0},{2,3},{3,2},{4,5},{5,4},{6,7},{7,6},{8,9},{9,8},{10,11... | collective-permute-start | bytes 786440 | tf_op jit(solution)/shard_map/ppermute | solution.py:18
  50.7 1.6 %collective-permute-start.10 = (f32[16,4096]{1,0:T(8,128)S(1)}, f32[16,4096]{1,0:T(8,128)S(1)}, u32[]{:S(2)}, u32[]{:S(2)}) collective-permute-start(f32[16,4096]{1,0:T(8,128)S(1)} %get-tuple-element.34), channel_id=1, source_target_pairs={{0,1},{1,0},{2,3},{3,2},{4,5},{5,4},{6,7},{7,6},{8,9},{9,8},{10,11... | collective-permute-start | bytes 786440 | tf_op jit(solution)/shard_map/ppermute | solution.py:18
where the time goes:
time: 53.7 us; the launch traced here: 53 us
  Pallas kernels  23.3 us (43%)
  starting transfers between devices  9.8 us (18%)
  waiting for transfers between devices  8.83 us (16%)
  other arithmetic  8.21 us (15%)
  between operations  1.53 us (3%)
  local copies, waits for them, and re-layouts  1.41 us (3%)
    pallas_call x5, Pallas kernels, tile_sum(): pl.pallas_call(lambda *refs: body(refs), out_shape=shapes, in_specs=in_sp...  22.5 us
    ppermute x11, starting transfers between devices, ring(): lax.ppermute(value, axis, [(i, (i + step) % size) for i in range(size)])  9.8 us
    ppermute x11, waiting for transfers between devices, ring(): lax.ppermute(value, axis, [(i, (i + step) % size) for i in range(size)])  8.83 us
    reduce_sum x2, other arithmetic, plan(): jnp.sum(jnp.where(position[:, None] == slot[None, :], (left * (slots + 1)...  2.41 us
    unnamed x4, local copies, waits for them, and re-layouts  1.16 us
  transfers between devices with their start and end apart: 11, of which 5 were waited for; matrix products, arithmetic and copies ran while one was open for 15% of the time, Pallas kernels for 25%

commit v1 on v0

--- a/solution.py
+++ b/solution.py
@@ -346,13 +346,6 @@
     key = jnp.where(place < square_count[0], moved_right(square_right), groups)
     chunks = -(-(tasks // CHUNK + groups + TURN * rows + TURN) // 16) * 16
     square_tasks = plan(key, left, square_out, groups, per_dev, slots, chunks)
-    from_col, left = moved_left(cube_left)
-    left = left - jnp.where(from_col == 0, 0, layers * per_dev)
-    key = jnp.where(from_col == 0, 0, groups) + moved_right(cube_right)
-    key = jnp.where(place < cube_count[0], key, 2 * groups)
-    chunks = -(-(tasks // CHUNK + 2 * groups + TURN * 2 + TURN) // 16) * 16
-    cube_tasks = plan(key, left, cube_out, 2 * groups, groups, slots, chunks)
-
     panel, first = prepare(lefts[:layers], column[:1])
     total, panel = tile_sum(
         square_tasks, 0, 1, lefts[layers:], [], panel, [first], None, False, slots, width, 0, True
@@ -369,6 +362,7 @@
         )
         total = result[0]
         weights.append(piece)
+
     if rows % 2 == 0:
         *result, piece = tile_sum(
             square_tasks, rows - 1, 1, [], [opposite], panel, [], total, True,
@@ -376,8 +370,19 @@
         )
         weights.append(piece)
     mine, other = result
+
     weights = jnp.concatenate(weights, axis=0)
     square = mine + ring(other, "depth")
+
+    cube_left, cube_right, cube_out, cube_count, square = lax.optimization_barrier(
+        (cube_left, cube_right, cube_out, cube_count, square)
+    )
+    from_col, left = moved_left(cube_left)
+    left = left - jnp.where(from_col == 0, 0, layers * per_dev)
+    key = jnp.where(from_col == 0, 0, groups) + moved_right(cube_right)
+    key = jnp.where(place < cube_count[0], key, 2 * groups)
+    chunks = -(-(tasks // CHUNK + 2 * groups + TURN * 2 + TURN) // 16) * 16
+    cube_tasks = plan(key, left, cube_out, 2 * groups, groups, slots, chunks)
 
     near = ring_all(square, "depth")
     far = ring_all(square, "col")[1:]

time: 53.7 us -> 53.7 us (level)
  the two profiles are of different devices: /device:TPU:5 before, /device:TPU:0 now
where the time goes in v1:
time: 53.7 us; the launch traced here: 53.6 us
  Pallas kernels  20 us (37%)
  starting transfers between devices  13.6 us (25%)
  waiting for transfers between devices  8.89 us (17%)
  other arithmetic  8.2 us (15%)
  between operations  1.59 us (3%)
  local copies, waits for them, and re-layouts  1.42 us (3%)
    pallas_call x5, Pallas kernels, tile_sum(): pl.pallas_call(lambda *refs: body(refs), out_shape=shapes, in_specs=in_sp...  19.2 us
    ppermute x11, starting transfers between devices, ring(): lax.ppermute(value, axis, [(i, (i + step) % size) for i in range(size)])  13.6 us
    ppermute x11, waiting for transfers between devices, ring(): lax.ppermute(value, axis, [(i, (i + step) % size) for i in range(size)])  8.89 us
    reduce_sum x2, other arithmetic, plan(): jnp.sum(jnp.where(position[:, None] == slot[None, :], (left * (slots + 1)...  2.41 us
    unnamed x10, local copies, waits for them, and re-layouts  1.18 us
  transfers between devices with their start and end apart: 11, of which 5 were waited for; matrix products, arithmetic and copies ran while one was open for 13% of the time, Pallas kernels for 22%

profile of v1, /device:TPU:0, one launch (start us, length us, event | category | flops | bytes accessed | tf_op | source)
XLA Modules:
  0.0 53.6 jit_solution(4999602128762523776)
XLA Ops:
  0.0 0.5 collective-permute-start.3
  0.5 2.5 %collective-permute-start.1 = (f32[16,4096]{1,0:T(8,128)}, f32[16,4096]{1,0:T(8,128)S(1)}, u32[]{:S(2)}, u32[]{:S(2)}) collective-permute-start(f32[16,4096]{1,0:T(8,128)} %refs_2_.1), channel_id=1, source_target_pairs={{0,2},{2,0},{1,3},{3,1},{4,6},{6,4},{5,7},{7,5},{8,10},{10,8},{9,1... | collective-permute-start | bytes 786440 | tf_op jit(solution)/shard_map/ppermute | solution.py:18
  2.9 1.6 %collective-permute-start = (f32[16,4096]{1,0:T(8,128)}, f32[16,4096]{1,0:T(8,128)S(1)}, u32[]{:S(2)}, u32[]{:S(2)}) collective-permute-start(f32[16,4096]{1,0:T(8,128)} %refs_2_.1), channel_id=1, source_target_pairs={{0,4},{4,8},{8,12},{12,0},{1,5},{5,9},{9,13},{13,1},{2,6},{6,10},{... | collective-permute-start | bytes 786440 | tf_op jit(solution)/shard_map/ppermute | solution.py:18
  4.5 2.2 %collective-permute-start.5 = (f32[16,4096]{1,0:T(8,128)}, f32[16,4096]{1,0:T(8,128)S(1)}, u32[]{:S(2)}, u32[]{:S(2)}) collective-permute-start(f32[16,4096]{1,0:T(8,128)} %refs_2_.1), channel_id=1, source_target_pairs={{0,12},{4,0},{8,4},{12,8},{1,13},{5,1},{9,5},{13,9},{2,14},{6,2},{... | collective-permute-start | bytes 786440 | tf_op jit(solution)/shard_map/ppermute | solution.py:18
  7.4 0.7 %fusion.14 = s32[1024]{0:T(1024)S(1)} fusion(s32[1024]{0:T(1024)} %param.11, s32[]{:T(128)S(6)} %axis_index.33, s32[]{:T(128)} %bitcast.2), kind=kLoop, calls=%fused_computation.91 | loop fusion | flops 39936 | bytes 8200 | tf_op jit(solution)/shard_map/jit(_where)/select_n | solution.py:346
  8.1 0.1 convert_reduce_fusion.3
  8.3 0.4 convert_reduce_fusion.1
  8.7 0.1 sub.165
  8.8 0.1 fusion.57
  8.9 0.1 select_reduce_fusion.7.refs_0_
  9.0 0.1 select_reduce_fusion.6
  9.1 0.1 select_reduce_fusion.5
  9.2 0.1 select_reduce_fusion.3
  9.3 0.7 %add_select_fusion.17 = s32[1024]{0:T(1024)S(1)} fusion(s32[1024]{0:T(1024)S(1)} %select_reduce_fusion.3, s32[1024]{0:T(1024)S(1)} %convert_reduce_fusion.1, s32[1024]{0:T(1024)} %param.11, s32[]{:T(128)S(6)} %axis_index.33, s32[]{:T(128)} %bitcast.3), kind=kLoop, calls=%fused_computation.132 | loop fusion | flops 43008 | bytes 16392 | tf_op jit(solution)/shard_map/jit(_where)/select_n | solution.py:48
  10.0 0.7 %fusion.55 = s32[1024]{0:T(1024)S(1)} fusion(s32[1024]{0:T(1024)} %param.12, s32[1024]{0:T(1024)} %param.10, s32[]{:T(128)S(6)} %axis_index.38, s32[]{:T(128)S(6)} %axis_index.36), kind=kLoop, calls=%fused_computation.140 | loop fusion | flops 64512 | bytes 12296 | tf_op jit(solution)/shard_map/sub | solution.py:52
  10.8 1.0 %select_reduce_fusion.1 = s32[1920]{0:T(1024)S(1)} fusion(s32[1024]{0:T(1024)S(1)} %fusion.55, s32[1024]{0:T(1024)S(1)} %add_select_fusion.17), kind=kLoop, calls=%fused_computation.2 | loop fusion | flops 5896320 | bytes 15872 | tf_op jit(solution)/shard_map/reduce_sum | solution.py:50
  11.8 0.0 collective-permute-done.1.refs_5_
  11.8 0.1 collective-permute-start.2
  11.9 0.1 convert_reduce_fusion.5.refs_2_
  12.0 0.0 collective-permute-done.3.refs_1_
  12.0 0.0 copy-start
  12.1 0.9 %copy-done = f32[16,4096]{1,0:T(8,128)S(1)} copy-done((f32[16,4096]{1,0:T(8,128)S(1)}, f32[16,4096]{1,0:T(8,128)}, u32[]{:S(2)}) %copy-start) | copy-done | bytes 262168
  13.0 0.8 %shard_map.91 = (bf16[2048,128]{1,0:T(8,128)(2,1)S(1)}, bf16[16,128,128]{2,1,0:T(8,128)(2,1)S(1)}) custom-call(f32[16,4096]{1,0:T(8,128)S(1)} %copy-done, f32[16,4096]{1,0:T(8,128)S(1)} %collective-permute-done.3.refs_1_, f32[16,4096]{1,0:T(8,128)S(1)} %copy-done), custom_call_target="tpu_custom_call" | custom-call | tf_op jit(solution)/shard_map/pallas_call | solution.py:120
  13.8 0.0 collective-permute-done.2.refs_6_
  13.8 2.9 %shard_map.92 = (f32[2112,128]{1,0:T(8,128)S(1)}, bf16[4096,128]{1,0:T(8,128)(2,1)S(1)}) custom-call(s32[4]{0:T(128)S(1)} %select_reduce_fusion.7.refs_0_, s32[4]{0:T(128)S(1)} %and_select_fusion.6.refs_1_, s32[240]{0:T(256)S(1)} %convert_reduce_fusion.5.refs_2_, s32[1920]{0:T(1024)S(1)} %get-tuple-element.48.refs_3_, s32[1920]{0:T(1024)S(1)} %get-tuple-element.47.refs_4_, ...), custom_call_target="tpu_custom_call" | custom-call | tf_op jit(solution)/shard_map/pallas_call | solution.py:290
  16.7 0.0 collective-permute-done.refs_5_
  16.7 0.8 %collective-permute-start.4 = (f32[16,4096]{1,0:T(8,128)S(1)}, f32[16,4096]{1,0:T(8,128)S(1)}, u32[]{:S(2)}, u32[]{:S(2)}) collective-permute-start(f32[16,4096]{1,0:T(8,128)S(1)} %collective-permute-done.refs_5_), channel_id=1, source_target_pairs={{0,4},{4,8},{8,12},{12,0},{1,5},{5,9},{9,13},{13,1},{2,6},{6,10},{... | collective-permute-start | bytes 786440 | tf_op jit(solution)/shard_map/ppermute | solution.py:18
  18.2 0.3 collective-permute-done.5.refs_6_
  18.5 3.3 %shard_map.93 = (f32[2112,128]{1,0:T(8,128)S(1)}, bf16[32,128,128]{2,1,0:T(8,128)(2,1)S(1)}) custom-call(s32[4]{0:T(128)S(1)} %select_reduce_fusion.7.refs_0_, s32[4]{0:T(128)S(1)} %and_select_fusion.6.refs_1_, s32[240]{0:T(256)S(1)} %convert_reduce_fusion.5.refs_2_, s32[1920]{0:T(1024)S(1)} %get-tuple-element.48.refs_3_, ...), custom_call_target="tpu_custom_call" | custom-call | tf_op jit(solution)/shard_map/pallas_call | solution.py:290
  21.8 5.0 %collective-permute-done.4.refs_5_ = f32[16,4096]{1,0:T(8,128)S(1)} collective-permute-done((f32[16,4096]{1,0:T(8,128)S(1)}, f32[16,4096]{1,0:T(8,128)S(1)}, u32[]{:S(2)}, u32[]{:S(2)}) %collective-permute-start.4) | collective-permute-done | bytes 262176 | tf_op jit(solution)/shard_map/ppermute | solution.py:18
  26.9 2.9 %shard_map.94 = (f32[16,4096]{1,0:T(8,128)S(1)}, f32[16,4096]{1,0:T(8,128)S(1)}, bf16[16,128,128]{2,1,0:T(8,128)(2,1)S(1)}) custom-call(s32[4]{0:T(128)S(1)} %select_reduce_fusion.7.refs_0_, s32[4]{0:T(128)S(1)} %and_select_fusion.6.refs_1_, s32[240]{0:T(256)S(1)} %convert_reduce_fusion.5.refs_2_, s32[1920]{0:T(1024)S(1)} %get-tuple-element.48.refs_3_, ...), custom_call_target="tpu_custom_call" | custom-call | tf_op jit(solution)/shard_map/pallas_call | solution.py:290
  29.8 0.0 copy-start.1
  29.8 0.0 copy-start.2
  29.8 0.0 copy-start.3
  29.8 0.1 collective-permute-start.6
  29.9 0.2 constant_dynamic-update-slice_fusion.1
  30.1 0.1 constant_dynamic-update-slice_fusion.refs_7_
  30.2 1.2 %collective-permute-done.6 = f32[16,4096]{1,0:T(8,128)S(1)} collective-permute-done((f32[16,4096]{1,0:T(8,128)S(1)}, f32[16,4096]{1,0:T(8,128)S(1)}, u32[]{:S(2)}, u32[]{:S(2)}) %collective-permute-start.6) | collective-permute-done | bytes 262176 | tf_op jit(solution)/shard_map/ppermute | solution.py:18
  31.5 0.0 copy-done.1
  31.5 0.0 copy-done.2
  31.5 0.0 copy-done.3
  31.5 0.2 convert_reduce_fusion.2
  31.8 0.4 convert_reduce_fusion
  32.2 0.2 collective-permute-start.7
  32.4 2.5 %collective-permute-start.8 = (f32[16,4096]{1,0:T(8,128)S(1)}, f32[16,4096]{1,0:T(8,128)S(1)}, u32[]{:S(2)}, u32[]{:S(2)}) collective-permute-start(f32[16,4096]{1,0:T(8,128)S(1)} %add.275.refs_5_), channel_id=1, source_target_pairs={{0,2},{2,0},{1,3},{3,1},{4,6},{6,4},{5,7},{7,5},{8,10},{10,8},{9,1... | collective-permute-start | bytes 786440 | tf_op jit(solution)/shard_map/ppermute | solution.py:18
  34.9 0.1 sub.189
  35.0 0.1 fusion.61
  35.1 0.1 fusion.59.refs_0_
  35.2 0.1 fusion.60
  35.3 0.1 select_reduce_fusion.4
  35.4 0.4 select_reduce_fusion.2
  35.8 1.4 %select_reduce_fusion = s32[2304]{0:T(1024)S(1)} fusion(s32[1024]{0:T(1024)S(1)} %get-tuple-element.49, s32[1024]{0:T(1024)S(1)} %add_select_fusion.16), kind=kLoop, calls=%fused_computation | loop fusion | flops 7075584 | bytes 17408 | tf_op jit(solution)/shard_map/reduce_sum | solution.py:50
  37.2 0.1 convert_reduce_fusion.4.refs_2_
  37.4 0.0 collective-permute-done.7.refs_6_
  37.4 4.7 %shard_map.95.refs_8_ = f32[2112,128]{1,0:T(8,128)S(1)} custom-call(s32[2]{0:T(128)S(1)} %fusion.59.refs_0_, s32[2]{0:T(128)S(1)} %and_select_fusion.2.refs_1_, s32[288]{0:T(512)S(1)} %convert_reduce_fusion.4.refs_2_, s32[2304]{0:T(1024)S(1)} %get-tuple-element.46.refs_3_, s32[2304]{0:T(1024)S(1)} %get-tuple-element.45.refs_4_, ...), custom_call_target="tpu_custom_call" | custom-call | tf_op jit(solution)/shard_map/pallas_call | solution.py:290
  42.1 0.0 collective-permute-done.8.refs_5_
  42.1 1.2 %collective-permute-start.9 = (f32[16,4096]{1,0:T(8,128)S(1)}, f32[16,4096]{1,0:T(8,128)S(1)}, u32[]{:S(2)}, u32[]{:S(2)}) collective-permute-start(f32[16,4096]{1,0:T(8,128)S(1)} %collective-permute-done.8.refs_5_), channel_id=1, source_target_pairs={{0,1},{1,0},{2,3},{3,2},{4,5},{5,4},{6,7},{7,6},{8,9},{9,8},{10,11... | collective-permute-start | bytes 786440 | tf_op jit(solution)/shard_map/ppermute | solution.py:18
  43.3 1.2 %collective-permute-done.9.refs_6_ = f32[16,4096]{1,0:T(8,128)S(1)} collective-permute-done((f32[16,4096]{1,0:T(8,128)S(1)}, f32[16,4096]{1,0:T(8,128)S(1)}, u32[]{:S(2)}, u32[]{:S(2)}) %collective-permute-start.9) | collective-permute-done | bytes 262176 | tf_op jit(solution)/shard_map/ppermute | solution.py:18
  44.5 5.3 %shard_map.96 = (f32[16,4096]{1,0:T(8,128)S(1)}, f32[16,4096]{1,0:T(8,128)S(1)}) custom-call(s32[2]{0:T(128)S(1)} %fusion.59.refs_0_, s32[2]{0:T(128)S(1)} %and_select_fusion.2.refs_1_, s32[288]{0:T(512)S(1)} %convert_reduce_fusion.4.refs_2_, s32[2304]{0:T(1024)S(1)} %get-tuple-element.46.refs_3_, s32[2304]{0:T(1024)S(1)} %get-tuple-element.45.refs_4_, ...), custom_call_target="tpu_custom_call" | custom-call | tf_op jit(solution)/shard_map/pallas_call | solution.py:290
  49.8 1.9 %collective-permute-start.10 = (f32[16,4096]{1,0:T(8,128)S(1)}, f32[16,4096]{1,0:T(8,128)S(1)}, u32[]{:S(2)}, u32[]{:S(2)}) collective-permute-start(f32[16,4096]{1,0:T(8,128)S(1)} %get-tuple-element.44), channel_id=1, source_target_pairs={{0,1},{1,0},{2,3},{3,2},{4,5},{5,4},{6,7},{7,6},{8,9},{9,8},{10,11... | collective-permute-start | bytes 786440 | tf_op jit(solution)/shard_map/ppermute | solution.py:18
  51.7 1.2 %collective-permute-done.10 = f32[16,4096]{1,0:T(8,128)S(1)} collective-permute-done((f32[16,4096]{1,0:T(8,128)S(1)}, f32[16,4096]{1,0:T(8,128)S(1)}, u32[]{:S(2)}, u32[]{:S(2)}) %collective-permute-start.10) | collective-permute-done | bytes 262176 | tf_op jit(solution)/shard_map/ppermute | solution.py:18
  52.9 0.8 %multiply_subtract_fusion = f32[16,4096]{1,0:T(8,128)} fusion(f32[16,4096]{1,0:T(8,128)S(1)} %get-tuple-element.43, f32[16,4096]{1,0:T(8,128)S(1)} %collective-permute-done.10, f32[16,4096]{1,0:T(8,128)S(1)} %add.275.refs_5_), kind=kLoop, calls=%fused_computation.12 | loop fusion | flops 262144 | bytes 1048576 | tf_op jit(solution)/shard_map/sub | solution.py:398
  (13 shorter events, 0.2 us)
Async XLA Ops:
  0.0 12.0 %collective-permute-start.3 = (f32[16,4096]{1,0:T(8,128)}, f32[16,4096]{1,0:T(8,128)S(1)}, u32[]{:S(2)}, u32[]{:S(2)}) collective-permute-start(f32[16,4096]{1,0:T(8,128)} %refs_2_.1), channel_id=1, source_target_pairs={{0,1},{1,0},{2,3},{3,2},{4,5},{5,4},{6,7},{7,6},{8,9},{9,8},{10,11... | collective-permute-start | bytes 786440 | tf_op jit(solution)/shard_map/ppermute | solution.py:18
  0.5 11.4 %collective-permute-start.1 = (f32[16,4096]{1,0:T(8,128)}, f32[16,4096]{1,0:T(8,128)S(1)}, u32[]{:S(2)}, u32[]{:S(2)}) collective-permute-start(f32[16,4096]{1,0:T(8,128)} %refs_2_.1), channel_id=1, source_target_pairs={{0,2},{2,0},{1,3},{3,1},{4,6},{6,4},{5,7},{7,5},{8,10},{10,8},{9,1... | collective-permute-start | bytes 786440 | tf_op jit(solution)/shard_map/ppermute | solution.py:18
  2.9 13.7 %collective-permute-start = (f32[16,4096]{1,0:T(8,128)}, f32[16,4096]{1,0:T(8,128)S(1)}, u32[]{:S(2)}, u32[]{:S(2)}) collective-permute-start(f32[16,4096]{1,0:T(8,128)} %refs_2_.1), channel_id=1, source_target_pairs={{0,4},{4,8},{8,12},{12,0},{1,5},{5,9},{9,13},{13,1},{2,6},{6,10},{... | collective-permute-start | bytes 786440 | tf_op jit(solution)/shard_map/ppermute | solution.py:18
  4.5 14.0 %collective-permute-start.5 = (f32[16,4096]{1,0:T(8,128)}, f32[16,4096]{1,0:T(8,128)S(1)}, u32[]{:S(2)}, u32[]{:S(2)}) collective-permute-start(f32[16,4096]{1,0:T(8,128)} %refs_2_.1), channel_id=1, source_target_pairs={{0,12},{4,0},{8,4},{12,8},{1,13},{5,1},{9,5},{13,9},{2,14},{6,2},{... | collective-permute-start | bytes 786440 | tf_op jit(solution)/shard_map/ppermute | solution.py:18
  11.8 1.9 %collective-permute-start.2 = (f32[16,4096]{1,0:T(8,128)S(1)}, f32[16,4096]{1,0:T(8,128)S(1)}, u32[]{:S(2)}, u32[]{:S(2)}) collective-permute-start(f32[16,4096]{1,0:T(8,128)S(1)} %collective-permute-done.1.refs_5_), channel_id=1, source_target_pairs={{0,1},{1,0},{2,3},{3,2},{4,5},{5,4},{6,7},{7,6},{8,9},{9,8},{10,11... | collective-permute-start | bytes 786440 | tf_op jit(solution)/shard_map/ppermute | solution.py:18
  12.0 1.0 %copy-start = (f32[16,4096]{1,0:T(8,128)S(1)}, f32[16,4096]{1,0:T(8,128)}, u32[]{:S(2)}) copy-start(f32[16,4096]{1,0:T(8,128)} %refs_2_.1) | copy-start | bytes 786436
  16.7 10.2 %collective-permute-start.4 = (f32[16,4096]{1,0:T(8,128)S(1)}, f32[16,4096]{1,0:T(8,128)S(1)}, u32[]{:S(2)}, u32[]{:S(2)}) collective-permute-start(f32[16,4096]{1,0:T(8,128)S(1)} %collective-permute-done.refs_5_), channel_id=1, source_target_pairs={{0,4},{4,8},{8,12},{12,0},{1,5},{5,9},{9,13},{13,1},{2,6},{6,10},{... | collective-permute-start | bytes 786440 | tf_op jit(solution)/shard_map/ppermute | solution.py:18
  29.8 1.7 %copy-start.1 = (s32[1024]{0:T(1024)S(1)}, s32[1024]{0:T(1024)}, u32[]{:S(2)}) copy-start(s32[1024]{0:T(1024)} %param.16) | copy-start | bytes 12292
  29.8 1.7 %copy-start.2 = (s32[1024]{0:T(1024)S(1)}, s32[1024]{0:T(1024)}, u32[]{:S(2)}) copy-start(s32[1024]{0:T(1024)} %param.14) | copy-start | bytes 12292
  29.8 1.7 %copy-start.3 = (s32[1024]{0:T(1024)S(1)}, s32[1024]{0:T(1024)}, u32[]{:S(2)}) copy-start(s32[1024]{0:T(1024)} %param.15) | copy-start | bytes 12292
  29.8 1.6 %collective-permute-start.6 = (f32[16,4096]{1,0:T(8,128)S(1)}, f32[16,4096]{1,0:T(8,128)S(1)}, u32[]{:S(2)}, u32[]{:S(2)}) collective-permute-start(f32[16,4096]{1,0:T(8,128)S(1)} %get-tuple-element.33), channel_id=1, source_target_pairs={{0,1},{1,0},{2,3},{3,2},{4,5},{5,4},{6,7},{7,6},{8,9},{9,8},{10,11... | collective-permute-start | bytes 786440 | tf_op jit(solution)/shard_map/ppermute | solution.py:18
  32.2 5.2 %collective-permute-start.7 = (f32[16,4096]{1,0:T(8,128)S(1)}, f32[16,4096]{1,0:T(8,128)S(1)}, u32[]{:S(2)}, u32[]{:S(2)}) collective-permute-start(f32[16,4096]{1,0:T(8,128)S(1)} %add.275.refs_5_), channel_id=1, source_target_pairs={{0,1},{1,0},{2,3},{3,2},{4,5},{5,4},{6,7},{7,6},{8,9},{9,8},{10,11... | collective-permute-start | bytes 786440 | tf_op jit(solution)/shard_map/ppermute | solution.py:18
  32.4 9.7 %collective-permute-start.8 = (f32[16,4096]{1,0:T(8,128)S(1)}, f32[16,4096]{1,0:T(8,128)S(1)}, u32[]{:S(2)}, u32[]{:S(2)}) collective-permute-start(f32[16,4096]{1,0:T(8,128)S(1)} %add.275.refs_5_), channel_id=1, source_target_pairs={{0,2},{2,0},{1,3},{3,1},{4,6},{6,4},{5,7},{7,5},{8,10},{10,8},{9,1... | collective-permute-start | bytes 786440 | tf_op jit(solution)/shard_map/ppermute | solution.py:18
  42.1 2.4 %collective-permute-start.9 = (f32[16,4096]{1,0:T(8,128)S(1)}, f32[16,4096]{1,0:T(8,128)S(1)}, u32[]{:S(2)}, u32[]{:S(2)}) collective-permute-start(f32[16,4096]{1,0:T(8,128)S(1)} %collective-permute-done.8.refs_5_), channel_id=1, source_target_pairs={{0,1},{1,0},{2,3},{3,2},{4,5},{5,4},{6,7},{7,6},{8,9},{9,8},{10,11... | collective-permute-start | bytes 786440 | tf_op jit(solution)/shard_map/ppermute | solution.py:18
  49.8 3.0 %collective-permute-start.10 = (f32[16,4096]{1,0:T(8,128)S(1)}, f32[16,4096]{1,0:T(8,128)S(1)}, u32[]{:S(2)}, u32[]{:S(2)}) collective-permute-start(f32[16,4096]{1,0:T(8,128)S(1)} %get-tuple-element.44), channel_id=1, source_target_pairs={{0,1},{1,0},{2,3},{3,2},{4,5},{5,4},{6,7},{7,6},{8,9},{9,8},{10,11... | collective-permute-start | bytes 786440 | tf_op jit(solution)/shard_map/ppermute | solution.py:18

commit v2 on v1

--- a/solution.py
+++ b/solution.py
@@ -94,7 +94,7 @@
             panel[pl.ds(row + 32, 32), :] = odd.astype(jnp.bfloat16)
 
 
-def fill_weights(sources, weights, flat, tall):
+def fill_weights(sources, weights, first, flat, tall):
     low, low_tall = low_half(32), low_half(64)
     for index, source in enumerate(sources):
         spread(source, flat)
@@ -105,14 +105,21 @@
             tall[pl.ds(spot, 32, stride=2), :] = jnp.where(low, both, swapped)
             tall[pl.ds(spot + 1, 32, stride=2), :] = jnp.where(low, swapped, both)
             top, rest = split(tall[spot : spot + 64, :])
-            weights[index * 16 + block, 0:64] = jnp.where(low_tall, top, rest).astype(jnp.bfloat16)
-            weights[index * 16 + block, 64:128] = jnp.where(low_tall, top, 0.0).astype(jnp.bfloat16)
+            weights[first + index * 16 + block, 0:64] = jnp.where(low_tall, top, rest).astype(jnp.bfloat16)
+            weights[first + index * 16 + block, 64:128] = jnp.where(low_tall, top, 0.0).astype(jnp.bfloat16)
 
 
 def prepare_kernel(raw_lefts, *refs):
     sources, (panel, weights, flat, tall) = refs[:-4], refs[-4:]
     fill_panel(sources[:raw_lefts], panel, 0, flat)
-    fill_weights(sources[raw_lefts:], weights, flat, tall)
+    fill_weights(sources[raw_lefts:], weights, 0, flat, tall)
+
+
+def extend_kernel(known, *refs):
+    sources, (panel, flat) = refs[:-2], refs[-2:]
+    size = known.shape[0]
+    panel[:size, :] = known[...]
+    fill_panel(sources, panel, size // 1024, flat)
 
 
 def prepare(lefts, rights):
@@ -128,6 +135,19 @@
         scratch_shapes=[pltpu.VMEM((size, 128), jnp.float32) for size in (512, 256)],
         compiler_params=pltpu.CompilerParams(vmem_limit_bytes=44 << 20),
     )(*lefts, *rights)
+
+
+def extend(panel, lefts):
+    vmem = pl.BlockSpec(memory_space=pltpu.VMEM)
+    rows = panel.shape[0] + len(lefts) * 1024
+    return pl.pallas_call(
+        extend_kernel,
+        out_shape=jax.ShapeDtypeStruct((rows, 128), jnp.bfloat16),
+        in_specs=[vmem] * (1 + len(lefts)),
+        out_specs=vmem,
+        scratch_shapes=[pltpu.VMEM((512, 128), jnp.float32)],
+        compiler_params=pltpu.CompilerParams(vmem_limit_bytes=44 << 20),
+    )(panel, *lefts)
 
 
 def kernel(raw_lefts, raw_rights, has_left, has_right, has_sum, last, slots, first_group, segs, keep, refs):
@@ -154,7 +174,11 @@
     weights = refs[0] if raw_rights else given[0]
     sums = (sum_0, sum_1)
     fill_panel(left_raw, panel, start, flat)
-    fill_weights(right_raw, weights, flat, tall)
+    known = 0
+    if raw_rights and has_right:
+        known = given[0].shape[0]
+        weights[:known] = given[0][...]
+    fill_weights(right_raw, weights, known, flat, tall)
 
     sum_1[...] = jnp.zeros_like(sum_1)
     if has_sum:
@@ -273,7 +297,8 @@
     elif left_raw:
         scratch = [pltpu.VMEM((blocks, 128), bf16)]
     if right_raw:
-        shapes.append(jax.ShapeDtypeStruct((len(right_raw) * 16, 128, 128), bf16))
+        blocks = len(right_raw) * 16 + sum(value.shape[0] for value in given)
+        shapes.append(jax.ShapeDtypeStruct((blocks, 128, 128), bf16))
     body = functools.partial(
         kernel,
         len(left_raw),
@@ -347,22 +372,20 @@
     chunks = -(-(tasks // CHUNK + groups + TURN * rows + TURN) // 16) * 16
     square_tasks = plan(key, left, square_out, groups, per_dev, slots, chunks)
     panel, first = prepare(lefts[:layers], column[:1])
-    total, panel = tile_sum(
-        square_tasks, 0, 1, lefts[layers:], [], panel, [first], None, False, slots, width, 0, True
-    )
-    weights = [first]
+    panel = extend(panel, lefts[layers:])
     if rows % 2 == 0:
-        column[-2], total = lax.optimization_barrier((column[-2], total))
+        column[-2], panel = lax.optimization_barrier((column[-2], panel))
         opposite = ring(column[-2] if rows > 2 else density, "row")
+    total, known, weights = None, [first], []
     for seg in range(1, len(column), 2):
         last = rows % 2 == 1 and seg + 2 == rows
+        begin = seg - len(known)
         *result, piece = tile_sum(
-            square_tasks, seg, 2, [], column[seg : seg + 2], panel, [], total, last,
-            slots, width, seg * per_dev,
+            square_tasks, begin, seg + 2 - begin, [], column[seg : seg + 2], panel, known, total,
+            last, slots, width, begin * per_dev,
         )
-        total = result[0]
+        total, known = result[0], []
         weights.append(piece)
-
     if rows % 2 == 0:
         *result, piece = tile_sum(
             square_tasks, rows - 1, 1, [], [opposite], panel, [], total, True,

time: 53.7 us -> 52.6 us (0.980)
  Pallas kernels: 20 us -> 26 us
  starting transfers between devices: 13.6 us -> 8.29 us
  waiting for transfers between devices: 8.89 us -> 6.86 us
    pallas_call x5 -> x4, Pallas kernels: 19.2 us -> 24.8 us  [tile_sum(): pl.pallas_call(lambda *refs: body(refs), out_shape=shapes, in_specs=in_sp...]
    ppermute x11, starting transfers between devices: 13.6 us -> 8.29 us  [ring(): lax.ppermute(value, axis, [(i, (i + step) % size) for i in range(size)])]
    ppermute x11, waiting for transfers between devices: 8.89 us -> 6.86 us  [ring(): lax.ppermute(value, axis, [(i, (i + step) % size) for i in range(size)])]
    unnamed x10 -> x9, local copies, waits for them, and re-layouts: 1.18 us -> 1.07 us
  transfers between devices with their start and end apart: 11 -> 11, of which waited for: 5 -> 4; matrix products, arithmetic and copies ran while one was open for 13% -> 14% of each run, Pallas kernels for 22% -> 29%
where the time goes in v2:
time: 52.6 us; the launch traced here: 52.3 us
  Pallas kernels  26 us (49%)
  starting transfers between devices  8.29 us (16%)
  other arithmetic  8.2 us (16%)
  waiting for transfers between devices  6.86 us (13%)
  between operations  1.6 us (3%)
  local copies, waits for them, and re-layouts  1.31 us (2%)
    pallas_call x4, Pallas kernels, tile_sum(): pl.pallas_call(lambda *refs: body(refs), out_shape=shapes, in_specs=in_sp...  24.8 us
    ppermute x11, starting transfers between devices, ring(): lax.ppermute(value, axis, [(i, (i + step) % size) for i in range(size)])  8.29 us
    ppermute x11, waiting for transfers between devices, ring(): lax.ppermute(value, axis, [(i, (i + step) % size) for i in range(size)])  6.86 us
    reduce_sum x2, other arithmetic, plan(): jnp.sum(jnp.where(position[:, None] == slot[None, :], (left * (slots + 1)...  2.41 us
    unnamed x9, local copies, waits for them, and re-layouts  1.07 us
  transfers between devices with their start and end apart: 11, of which 4 were waited for; matrix products, arithmetic and copies ran while one was open for 14% of the time, Pallas kernels for 29%

profile of v2, /device:TPU:0, one launch (start us, length us, event | category | flops | bytes accessed | tf_op | source)
XLA Modules:
  0.0 52.3 jit_solution(717375469957700315)
XLA Ops:
  0.0 0.5 collective-permute-start.1
  0.5 2.5 %collective-permute-start.2 = (f32[16,4096]{1,0:T(8,128)}, f32[16,4096]{1,0:T(8,128)S(1)}, u32[]{:S(2)}, u32[]{:S(2)}) collective-permute-start(f32[16,4096]{1,0:T(8,128)} %refs_2_.1), channel_id=1, source_target_pairs={{0,2},{2,0},{1,3},{3,1},{4,6},{6,4},{5,7},{7,5},{8,10},{10,8},{9,1... | collective-permute-start | bytes 786440 | tf_op jit(solution)/shard_map/ppermute | solution.py:18
  2.9 1.6 %collective-permute-start = (f32[16,4096]{1,0:T(8,128)}, f32[16,4096]{1,0:T(8,128)S(1)}, u32[]{:S(2)}, u32[]{:S(2)}) collective-permute-start(f32[16,4096]{1,0:T(8,128)} %refs_2_.1), channel_id=1, source_target_pairs={{0,4},{4,8},{8,12},{12,0},{1,5},{5,9},{9,13},{13,1},{2,6},{6,10},{... | collective-permute-start | bytes 786440 | tf_op jit(solution)/shard_map/ppermute | solution.py:18
  4.5 2.2 %collective-permute-start.5 = (f32[16,4096]{1,0:T(8,128)}, f32[16,4096]{1,0:T(8,128)S(1)}, u32[]{:S(2)}, u32[]{:S(2)}) collective-permute-start(f32[16,4096]{1,0:T(8,128)} %refs_2_.1), channel_id=1, source_target_pairs={{0,12},{4,0},{8,4},{12,8},{1,13},{5,1},{9,5},{13,9},{2,14},{6,2},{... | collective-permute-start | bytes 786440 | tf_op jit(solution)/shard_map/ppermute | solution.py:18
  7.4 0.7 %fusion.14 = s32[1024]{0:T(1024)S(1)} fusion(s32[1024]{0:T(1024)} %param.11, s32[]{:T(128)S(6)} %axis_index.33, s32[]{:T(128)} %bitcast.2), kind=kLoop, calls=%fused_computation.90 | loop fusion | flops 39936 | bytes 8200 | tf_op jit(solution)/shard_map/jit(_where)/select_n | solution.py:371
  8.1 0.1 convert_reduce_fusion.3
  8.3 0.4 convert_reduce_fusion.1
  8.7 0.1 sub.165
  8.8 0.1 fusion.57
  8.9 0.1 select_reduce_fusion.7.refs_0_
  9.0 0.1 select_reduce_fusion.6
  9.1 0.1 select_reduce_fusion.5
  9.2 0.1 select_reduce_fusion.3
  9.3 0.7 %fusion.55 = s32[1024]{0:T(1024)S(1)} fusion(s32[1024]{0:T(1024)} %param.12, s32[1024]{0:T(1024)} %param.10, s32[]{:T(128)S(6)} %axis_index.38, s32[]{:T(128)S(6)} %axis_index.36), kind=kLoop, calls=%fused_computation.139 | loop fusion | flops 64512 | bytes 12296 | tf_op jit(solution)/shard_map/sub | solution.py:52
  10.1 0.1 convert_reduce_fusion.5.refs_2_
  10.2 0.7 %add_select_fusion.17 = s32[1024]{0:T(1024)S(1)} fusion(s32[1024]{0:T(1024)S(1)} %select_reduce_fusion.3, s32[1024]{0:T(1024)S(1)} %convert_reduce_fusion.1, s32[1024]{0:T(1024)} %param.11, s32[]{:T(128)S(6)} %axis_index.33, s32[]{:T(128)} %bitcast.3), kind=kLoop, calls=%fused_computation.131 | loop fusion | flops 43008 | bytes 16392 | tf_op jit(solution)/shard_map/jit(_where)/select_n | solution.py:48
  10.9 0.0 collective-permute-done.2.refs_0_
  10.9 0.1 collective-permute-start.3
  11.0 1.0 %select_reduce_fusion.1 = s32[1920]{0:T(1024)S(1)} fusion(s32[1024]{0:T(1024)S(1)} %fusion.55, s32[1024]{0:T(1024)S(1)} %add_select_fusion.17), kind=kLoop, calls=%fused_computation.2 | loop fusion | flops 5896320 | bytes 15872 | tf_op jit(solution)/shard_map/reduce_sum | solution.py:50
  12.0 0.0 collective-permute-done.1.refs_1_
  12.0 0.0 copy-start
  12.0 0.9 %copy-done = f32[16,4096]{1,0:T(8,128)S(1)} copy-done((f32[16,4096]{1,0:T(8,128)S(1)}, f32[16,4096]{1,0:T(8,128)}, u32[]{:S(2)}) %copy-start) | copy-done | bytes 262168
  13.0 0.8 %shard_map.91 = (bf16[2048,128]{1,0:T(8,128)(2,1)S(1)}, bf16[16,128,128]{2,1,0:T(8,128)(2,1)S(1)}) custom-call(f32[16,4096]{1,0:T(8,128)S(1)} %copy-done, f32[16,4096]{1,0:T(8,128)S(1)} %collective-permute-done.1.refs_1_, f32[16,4096]{1,0:T(8,128)S(1)} %copy-done), custom_call_target="tpu_custom_call" | custom-call | tf_op jit(solution)/shard_map/pallas_call | solution.py:127
  13.7 0.0 collective-permute-done.3.refs_1_
  13.8 0.5 shard_map.92.refs_7_.refs_6_
  14.3 0.0 collective-permute-done.refs_5_
  14.3 1.0 %collective-permute-start.4 = (f32[16,4096]{1,0:T(8,128)S(1)}, f32[16,4096]{1,0:T(8,128)S(1)}, u32[]{:S(2)}, u32[]{:S(2)}) collective-permute-start(f32[16,4096]{1,0:T(8,128)S(1)} %collective-permute-done.refs_5_), channel_id=1, source_target_pairs={{0,4},{4,8},{8,12},{12,0},{1,5},{5,9},{9,13},{13,1},{2,6},{6,10},{... | collective-permute-start | bytes 786440 | tf_op jit(solution)/shard_map/ppermute | solution.py:18
  16.0 2.5 %collective-permute-done.5.refs_6_ = f32[16,4096]{1,0:T(8,128)S(1)} collective-permute-done((f32[16,4096]{1,0:T(8,128)}, f32[16,4096]{1,0:T(8,128)S(1)}, u32[]{:S(2)}, u32[]{:S(2)}) %collective-permute-start.5) | collective-permute-done | bytes 262176 | tf_op jit(solution)/shard_map/ppermute | solution.py:18
  18.5 7.8 %shard_map.93 = (f32[2112,128]{1,0:T(8,128)S(1)}, bf16[48,128,128]{2,1,0:T(8,128)(2,1)S(1)}) custom-call(s32[4]{0:T(128)S(1)} %select_reduce_fusion.7.refs_0_, s32[4]{0:T(128)S(1)} %and_select_fusion.6.refs_1_, s32[240]{0:T(256)S(1)} %convert_reduce_fusion.5.refs_2_, s32[1920]{0:T(1024)S(1)} %get-tuple-element.44.refs_3_, ...), custom_call_target="tpu_custom_call" | custom-call | tf_op jit(solution)/shard_map/pallas_call | solution.py:315
  26.3 0.0 collective-permute-done.4.refs_5_
  26.3 4.0 %shard_map.94 = (f32[16,4096]{1,0:T(8,128)S(1)}, f32[16,4096]{1,0:T(8,128)S(1)}, bf16[16,128,128]{2,1,0:T(8,128)(2,1)S(1)}) custom-call(s32[4]{0:T(128)S(1)} %select_reduce_fusion.7.refs_0_, s32[4]{0:T(128)S(1)} %and_select_fusion.6.refs_1_, s32[240]{0:T(256)S(1)} %convert_reduce_fusion.5.refs_2_, s32[1920]{0:T(1024)S(1)} %get-tuple-element.44.refs_3_, ...), custom_call_target="tpu_custom_call" | custom-call | tf_op jit(solution)/shard_map/pallas_call | solution.py:315
  30.4 0.1 collective-permute-start.6
  30.4 0.0 copy-start.1
  30.5 0.0 copy-start.2
  30.5 0.0 copy-start.3
  30.5 0.1 constant_dynamic-update-slice_fusion.1
  30.6 0.1 constant_dynamic-update-slice_fusion.refs_7_
  30.7 1.3 %collective-permute-done.6 = f32[16,4096]{1,0:T(8,128)S(1)} collective-permute-done((f32[16,4096]{1,0:T(8,128)S(1)}, f32[16,4096]{1,0:T(8,128)S(1)}, u32[]{:S(2)}, u32[]{:S(2)}) %collective-permute-start.6) | collective-permute-done | bytes 262176 | tf_op jit(solution)/shard_map/ppermute | solution.py:18
  32.0 0.0 copy-done.1
  32.0 0.0 copy-done.2
  32.0 0.0 copy-done.3
  32.1 0.2 convert_reduce_fusion.2
  32.3 0.4 convert_reduce_fusion
  32.7 0.2 collective-permute-start.7
  32.9 0.0 collective-permute-start.8
  32.9 0.1 sub.189
  33.0 0.1 fusion.61
  33.1 0.1 fusion.59.refs_0_
  33.2 0.1 fusion.60
  33.3 0.1 select_reduce_fusion.4
  33.4 0.4 select_reduce_fusion.2
  33.8 1.4 %select_reduce_fusion = s32[2304]{0:T(1024)S(1)} fusion(s32[1024]{0:T(1024)S(1)} %get-tuple-element.45, s32[1024]{0:T(1024)S(1)} %add_select_fusion.16), kind=kLoop, calls=%fused_computation | loop fusion | flops 7075584 | bytes 17408 | tf_op jit(solution)/shard_map/reduce_sum | solution.py:50
  35.2 0.1 convert_reduce_fusion.4.refs_2_
  35.4 0.0 collective-permute-done.7.refs_6_
  35.4 6.2 %shard_map.95.refs_8_ = f32[2112,128]{1,0:T(8,128)S(1)} custom-call(s32[2]{0:T(128)S(1)} %fusion.59.refs_0_, s32[2]{0:T(128)S(1)} %and_select_fusion.2.refs_1_, s32[288]{0:T(512)S(1)} %convert_reduce_fusion.4.refs_2_, s32[2304]{0:T(1024)S(1)} %get-tuple-element.42.refs_3_, s32[2304]{0:T(1024)S(1)} %get-tuple-element.41.refs_4_, ...), custom_call_target="tpu_custom_call" | custom-call | tf_op jit(solution)/shard_map/pallas_call | solution.py:315
  41.6 0.0 collective-permute-done.8.refs_5_
  41.6 0.1 collective-permute-start.9
  41.7 1.5 %collective-permute-done.9.refs_6_ = f32[16,4096]{1,0:T(8,128)S(1)} collective-permute-done((f32[16,4096]{1,0:T(8,128)S(1)}, f32[16,4096]{1,0:T(8,128)S(1)}, u32[]{:S(2)}, u32[]{:S(2)}) %collective-permute-start.9) | collective-permute-done | bytes 262176 | tf_op jit(solution)/shard_map/ppermute | solution.py:18
  43.2 6.8 %shard_map.96 = (f32[16,4096]{1,0:T(8,128)S(1)}, f32[16,4096]{1,0:T(8,128)S(1)}) custom-call(s32[2]{0:T(128)S(1)} %fusion.59.refs_0_, s32[2]{0:T(128)S(1)} %and_select_fusion.2.refs_1_, s32[288]{0:T(512)S(1)} %convert_reduce_fusion.4.refs_2_, s32[2304]{0:T(1024)S(1)} %get-tuple-element.42.refs_3_, s32[2304]{0:T(1024)S(1)} %get-tuple-element.41.refs_4_, ...), custom_call_target="tpu_custom_call" | custom-call | tf_op jit(solution)/shard_map/pallas_call | solution.py:315
  50.0 0.1 collective-permute-start.10
  50.0 1.5 %collective-permute-done.10 = f32[16,4096]{1,0:T(8,128)S(1)} collective-permute-done((f32[16,4096]{1,0:T(8,128)S(1)}, f32[16,4096]{1,0:T(8,128)S(1)}, u32[]{:S(2)}, u32[]{:S(2)}) %collective-permute-start.10) | collective-permute-done | bytes 262176 | tf_op jit(solution)/shard_map/ppermute | solution.py:18
  51.6 0.8 %multiply_subtract_fusion = f32[16,4096]{1,0:T(8,128)} fusion(f32[16,4096]{1,0:T(8,128)S(1)} %get-tuple-element.39, f32[16,4096]{1,0:T(8,128)S(1)} %collective-permute-done.10, f32[16,4096]{1,0:T(8,128)S(1)} %add.275.refs_5_), kind=kLoop, calls=%fused_computation.12 | loop fusion | flops 262144 | bytes 1048576 | tf_op jit(solution)/shard_map/sub | solution.py:421
  (12 shorter events, 0.2 us)
Async XLA Ops:
  0.0 12.0 %collective-permute-start.1 = (f32[16,4096]{1,0:T(8,128)}, f32[16,4096]{1,0:T(8,128)S(1)}, u32[]{:S(2)}, u32[]{:S(2)}) collective-permute-start(f32[16,4096]{1,0:T(8,128)} %refs_2_.1), channel_id=1, source_target_pairs={{0,1},{1,0},{2,3},{3,2},{4,5},{5,4},{6,7},{7,6},{8,9},{9,8},{10,11... | collective-permute-start | bytes 786440 | tf_op jit(solution)/shard_map/ppermute | solution.py:18
  0.5 10.4 %collective-permute-start.2 = (f32[16,4096]{1,0:T(8,128)}, f32[16,4096]{1,0:T(8,128)S(1)}, u32[]{:S(2)}, u32[]{:S(2)}) collective-permute-start(f32[16,4096]{1,0:T(8,128)} %refs_2_.1), channel_id=1, source_target_pairs={{0,2},{2,0},{1,3},{3,1},{4,6},{6,4},{5,7},{7,5},{8,10},{10,8},{9,1... | collective-permute-start | bytes 786440 | tf_op jit(solution)/shard_map/ppermute | solution.py:18
  2.9 11.3 %collective-permute-start = (f32[16,4096]{1,0:T(8,128)}, f32[16,4096]{1,0:T(8,128)S(1)}, u32[]{:S(2)}, u32[]{:S(2)}) collective-permute-start(f32[16,4096]{1,0:T(8,128)} %refs_2_.1), channel_id=1, source_target_pairs={{0,4},{4,8},{8,12},{12,0},{1,5},{5,9},{9,13},{13,1},{2,6},{6,10},{... | collective-permute-start | bytes 786440 | tf_op jit(solution)/shard_map/ppermute | solution.py:18
  4.5 14.0 %collective-permute-start.5 = (f32[16,4096]{1,0:T(8,128)}, f32[16,4096]{1,0:T(8,128)S(1)}, u32[]{:S(2)}, u32[]{:S(2)}) collective-permute-start(f32[16,4096]{1,0:T(8,128)} %refs_2_.1), channel_id=1, source_target_pairs={{0,12},{4,0},{8,4},{12,8},{1,13},{5,1},{9,5},{13,9},{2,14},{6,2},{... | collective-permute-start | bytes 786440 | tf_op jit(solution)/shard_map/ppermute | solution.py:18
  10.9 2.9 %collective-permute-start.3 = (f32[16,4096]{1,0:T(8,128)S(1)}, f32[16,4096]{1,0:T(8,128)S(1)}, u32[]{:S(2)}, u32[]{:S(2)}) collective-permute-start(f32[16,4096]{1,0:T(8,128)S(1)} %collective-permute-done.2.refs_0_), channel_id=1, source_target_pairs={{0,1},{1,0},{2,3},{3,2},{4,5},{5,4},{6,7},{7,6},{8,9},{9,8},{10,11... | collective-permute-start | bytes 786440 | tf_op jit(solution)/shard_map/ppermute | solution.py:18
  12.0 1.0 %copy-start = (f32[16,4096]{1,0:T(8,128)S(1)}, f32[16,4096]{1,0:T(8,128)}, u32[]{:S(2)}) copy-start(f32[16,4096]{1,0:T(8,128)} %refs_2_.1) | copy-start | bytes 786436
  14.3 12.0 %collective-permute-start.4 = (f32[16,4096]{1,0:T(8,128)S(1)}, f32[16,4096]{1,0:T(8,128)S(1)}, u32[]{:S(2)}, u32[]{:S(2)}) collective-permute-start(f32[16,4096]{1,0:T(8,128)S(1)} %collective-permute-done.refs_5_), channel_id=1, source_target_pairs={{0,4},{4,8},{8,12},{12,0},{1,5},{5,9},{9,13},{13,1},{2,6},{6,10},{... | collective-permute-start | bytes 786440 | tf_op jit(solution)/shard_map/ppermute | solution.py:18
  30.4 1.6 %collective-permute-start.6 = (f32[16,4096]{1,0:T(8,128)S(1)}, f32[16,4096]{1,0:T(8,128)S(1)}, u32[]{:S(2)}, u32[]{:S(2)}) collective-permute-start(f32[16,4096]{1,0:T(8,128)S(1)} %get-tuple-element.29), channel_id=1, source_target_pairs={{0,1},{1,0},{2,3},{3,2},{4,5},{5,4},{6,7},{7,6},{8,9},{9,8},{10,11... | collective-permute-start | bytes 786440 | tf_op jit(solution)/shard_map/ppermute | solution.py:18
  30.4 1.6 %copy-start.1 = (s32[1024]{0:T(1024)S(1)}, s32[1024]{0:T(1024)}, u32[]{:S(2)}) copy-start(s32[1024]{0:T(1024)} %param.16) | copy-start | bytes 12292
  30.5 1.6 %copy-start.2 = (s32[1024]{0:T(1024)S(1)}, s32[1024]{0:T(1024)}, u32[]{:S(2)}) copy-start(s32[1024]{0:T(1024)} %param.14) | copy-start | bytes 12292
  30.5 1.6 %copy-start.3 = (s32[1024]{0:T(1024)S(1)}, s32[1024]{0:T(1024)}, u32[]{:S(2)}) copy-start(s32[1024]{0:T(1024)} %param.15) | copy-start | bytes 12292
  32.7 2.7 %collective-permute-start.7 = (f32[16,4096]{1,0:T(8,128)S(1)}, f32[16,4096]{1,0:T(8,128)S(1)}, u32[]{:S(2)}, u32[]{:S(2)}) collective-permute-start(f32[16,4096]{1,0:T(8,128)S(1)} %add.275.refs_5_), channel_id=1, source_target_pairs={{0,1},{1,0},{2,3},{3,2},{4,5},{5,4},{6,7},{7,6},{8,9},{9,8},{10,11... | collective-permute-start | bytes 786440 | tf_op jit(solution)/shard_map/ppermute | solution.py:18
  32.9 8.7 %collective-permute-start.8 = (f32[16,4096]{1,0:T(8,128)S(1)}, f32[16,4096]{1,0:T(8,128)S(1)}, u32[]{:S(2)}, u32[]{:S(2)}) collective-permute-start(f32[16,4096]{1,0:T(8,128)S(1)} %add.275.refs_5_), channel_id=1, source_target_pairs={{0,2},{2,0},{1,3},{3,1},{4,6},{6,4},{5,7},{7,5},{8,10},{10,8},{9,1... | collective-permute-start | bytes 786440 | tf_op jit(solution)/shard_map/ppermute | solution.py:18
  41.6 1.6 %collective-permute-start.9 = (f32[16,4096]{1,0:T(8,128)S(1)}, f32[16,4096]{1,0:T(8,128)S(1)}, u32[]{:S(2)}, u32[]{:S(2)}) collective-permute-start(f32[16,4096]{1,0:T(8,128)S(1)} %collective-permute-done.8.refs_5_), channel_id=1, source_target_pairs={{0,1},{1,0},{2,3},{3,2},{4,5},{5,4},{6,7},{7,6},{8,9},{9,8},{10,11... | collective-permute-start | bytes 786440 | tf_op jit(solution)/shard_map/ppermute | solution.py:18
  50.0 1.6 %collective-permute-start.10 = (f32[16,4096]{1,0:T(8,128)S(1)}, f32[16,4096]{1,0:T(8,128)S(1)}, u32[]{:S(2)}, u32[]{:S(2)}) collective-permute-start(f32[16,4096]{1,0:T(8,128)S(1)} %get-tuple-element.40), channel_id=1, source_target_pairs={{0,1},{1,0},{2,3},{3,2},{4,5},{5,4},{6,7},{7,6},{8,9},{9,8},{10,11... | collective-permute-start | bytes 786440 | tf_op jit(solution)/shard_map/ppermute | solution.py:18

commit v3 on v2

--- a/solution.py
+++ b/solution.py
@@ -376,6 +376,16 @@
     if rows % 2 == 0:
         column[-2], panel = lax.optimization_barrier((column[-2], panel))
         opposite = ring(column[-2] if rows > 2 else density, "row")
+    cube_left, cube_right, cube_out, cube_count, panel = lax.optimization_barrier(
+        (cube_left, cube_right, cube_out, cube_count, panel)
+    )
+    from_col, left = moved_left(cube_left)
+    left = left - jnp.where(from_col == 0, 0, layers * per_dev)
+    key = jnp.where(from_col == 0, 0, groups) + moved_right(cube_right)
+    key = jnp.where(place < cube_count[0], key, 2 * groups)
+    chunks = -(-(tasks // CHUNK + 2 * groups + TURN * 2 + TURN) // 16) * 16
+    cube_tasks = plan(key, left, cube_out, 2 * groups, groups, slots, chunks)
+
     total, known, weights = None, [first], []
     for seg in range(1, len(column), 2):
         last = rows % 2 == 1 and seg + 2 == rows
@@ -397,16 +407,6 @@
     weights = jnp.concatenate(weights, axis=0)
     square = mine + ring(other, "depth")
 
-    cube_left, cube_right, cube_out, cube_count, square = lax.optimization_barrier(
-        (cube_left, cube_right, cube_out, cube_count, square)
-    )
-    from_col, left = moved_left(cube_left)
-    left = left - jnp.where(from_col == 0, 0, layers * per_dev)
-    key = jnp.where(from_col == 0, 0, groups) + moved_right(cube_right)
-    key = jnp.where(place < cube_count[0], key, 2 * groups)
-    chunks = -(-(tasks // CHUNK + 2 * groups + TURN * 2 + TURN) // 16) * 16
-    cube_tasks = plan(key, left, cube_out, 2 * groups, groups, slots, chunks)
-
     near = ring_all(square, "depth")
     far = ring_all(square, "col")[1:]
     (total,) = tile_sum(

time: 52.6 us -> 52 us (0.989)
  the two profiles are of different devices: /device:TPU:0 before, /device:TPU:9 now
where the time goes in v3:
time: 52 us; the launch traced here: 52.1 us
  Pallas kernels  16.2 us (31%)
  starting transfers between devices  14.7 us (28%)
  waiting for transfers between devices  10 us (19%)
  other arithmetic  8.18 us (16%)
  between operations  1.51 us (3%)
  local copies, waits for them, and re-layouts  1.37 us (3%)
    pallas_call x4, Pallas kernels, tile_sum(): pl.pallas_call(lambda *refs: body(refs), out_shape=shapes, in_specs=in_sp...  14.9 us
    ppermute x11, starting transfers between devices, ring(): lax.ppermute(value, axis, [(i, (i + step) % size) for i in range(size)])  14.7 us
    ppermute x11, waiting for transfers between devices, ring(): lax.ppermute(value, axis, [(i, (i + step) % size) for i in range(size)])  10 us
    reduce_sum x2, other arithmetic, plan(): jnp.sum(jnp.where(position[:, None] == slot[None, :], (left * (slots + 1)...  2.41 us
    unnamed x9, local copies, waits for them, and re-layouts  1.12 us
  transfers between devices with their start and end apart: 11, of which 7 were waited for; matrix products, arithmetic and copies ran while one was open for 15% of the time, Pallas kernels for 17%

profile of v3, /device:TPU:9, one launch (start us, length us, event | category | flops | bytes accessed | tf_op | source)
XLA Modules:
  0.0 52.1 jit_solution(6453059359863561221)
XLA Ops:
  0.0 0.0 copy-start.2
  0.0 0.0 copy-start.3
  0.0 0.0 copy-start.1
  0.0 1.3 %collective-permute-start = (f32[16,4096]{1,0:T(8,128)}, f32[16,4096]{1,0:T(8,128)S(1)}, u32[]{:S(2)}, u32[]{:S(2)}) collective-permute-start(f32[16,4096]{1,0:T(8,128)} %refs_2_.1), channel_id=1, source_target_pairs={{0,4},{4,8},{8,12},{12,0},{1,5},{5,9},{9,13},{13,1},{2,6},{6,10},{... | collective-permute-start | bytes 786440 | tf_op jit(solution)/shard_map/ppermute | solution.py:18
  1.4 1.0 %collective-permute-start.1 = (f32[16,4096]{1,0:T(8,128)}, f32[16,4096]{1,0:T(8,128)S(1)}, u32[]{:S(2)}, u32[]{:S(2)}) collective-permute-start(f32[16,4096]{1,0:T(8,128)} %refs_2_.1), channel_id=1, source_target_pairs={{0,1},{1,0},{2,3},{3,2},{4,5},{5,4},{6,7},{7,6},{8,9},{9,8},{10,11... | collective-permute-start | bytes 786440 | tf_op jit(solution)/shard_map/ppermute | solution.py:18
  2.3 1.2 %collective-permute-start.2 = (f32[16,4096]{1,0:T(8,128)}, f32[16,4096]{1,0:T(8,128)S(1)}, u32[]{:S(2)}, u32[]{:S(2)}) collective-permute-start(f32[16,4096]{1,0:T(8,128)} %refs_2_.1), channel_id=1, source_target_pairs={{0,2},{2,0},{1,3},{3,1},{4,6},{6,4},{5,7},{7,5},{8,10},{10,8},{9,1... | collective-permute-start | bytes 786440 | tf_op jit(solution)/shard_map/ppermute | solution.py:18
  3.5 0.2 collective-permute-start.5
  4.3 0.7 %fusion.14 = s32[1024]{0:T(1024)S(1)} fusion(s32[1024]{0:T(1024)} %param.11, s32[]{:T(128)S(6)} %axis_index.33, s32[]{:T(128)} %bitcast.2), kind=kLoop, calls=%fused_computation.90 | loop fusion | flops 39936 | bytes 8200 | tf_op jit(solution)/shard_map/jit(_where)/select_n | solution.py:371
  5.1 0.1 convert_reduce_fusion.3
  5.2 0.4 convert_reduce_fusion.1
  5.6 0.1 sub.165
  5.7 0.1 fusion.57
  5.8 0.1 select_reduce_fusion.7.refs_0_
  5.9 0.1 select_reduce_fusion.5
  6.0 0.1 select_reduce_fusion.6
  6.1 0.1 select_reduce_fusion.3
  6.2 0.7 %add_select_fusion.17 = s32[1024]{0:T(1024)S(1)} fusion(s32[1024]{0:T(1024)S(1)} %select_reduce_fusion.3, s32[1024]{0:T(1024)S(1)} %convert_reduce_fusion.1, s32[1024]{0:T(1024)} %param.11, s32[]{:T(128)S(6)} %axis_index.33, s32[]{:T(128)} %bitcast.3), kind=kLoop, calls=%fused_computation.131 | loop fusion | flops 43008 | bytes 16392 | tf_op jit(solution)/shard_map/jit(_where)/select_n | solution.py:48
  7.0 0.7 %fusion.55 = s32[1024]{0:T(1024)S(1)} fusion(s32[1024]{0:T(1024)} %param.12, s32[1024]{0:T(1024)} %param.10, s32[]{:T(128)S(6)} %axis_index.38, s32[]{:T(128)S(6)} %axis_index.36), kind=kLoop, calls=%fused_computation.139 | loop fusion | flops 64512 | bytes 12296 | tf_op jit(solution)/shard_map/sub | solution.py:52
  7.7 1.0 %select_reduce_fusion.1 = s32[1920]{0:T(1024)S(1)} fusion(s32[1024]{0:T(1024)S(1)} %fusion.55, s32[1024]{0:T(1024)S(1)} %add_select_fusion.17), kind=kLoop, calls=%fused_computation.2 | loop fusion | flops 5896320 | bytes 15872 | tf_op jit(solution)/shard_map/reduce_sum | solution.py:50
  8.7 1.7 %collective-permute-done.2.refs_0_ = f32[16,4096]{1,0:T(8,128)S(1)} collective-permute-done((f32[16,4096]{1,0:T(8,128)}, f32[16,4096]{1,0:T(8,128)S(1)}, u32[]{:S(2)}, u32[]{:S(2)}) %collective-permute-start.2) | collective-permute-done | bytes 262176 | tf_op jit(solution)/shard_map/ppermute | solution.py:18
  10.5 0.8 %collective-permute-start.3 = (f32[16,4096]{1,0:T(8,128)S(1)}, f32[16,4096]{1,0:T(8,128)S(1)}, u32[]{:S(2)}, u32[]{:S(2)}) collective-permute-start(f32[16,4096]{1,0:T(8,128)S(1)} %collective-permute-done.2.refs_0_), channel_id=1, source_target_pairs={{0,1},{1,0},{2,3},{3,2},{4,5},{5,4},{6,7},{7,6},{8,9},{9,8},{10,11... | collective-permute-start | bytes 786440 | tf_op jit(solution)/shard_map/ppermute | solution.py:18
  11.2 0.1 convert_reduce_fusion.5.refs_2_
  12.0 0.0 collective-permute-done.1.refs_1_
  12.0 0.0 copy-start
  12.0 0.9 %copy-done = f32[16,4096]{1,0:T(8,128)S(1)} copy-done((f32[16,4096]{1,0:T(8,128)S(1)}, f32[16,4096]{1,0:T(8,128)}, u32[]{:S(2)}) %copy-start) | copy-done | bytes 262168
  13.0 0.8 %shard_map.91 = (bf16[2048,128]{1,0:T(8,128)(2,1)S(1)}, bf16[16,128,128]{2,1,0:T(8,128)(2,1)S(1)}) custom-call(f32[16,4096]{1,0:T(8,128)S(1)} %copy-done, f32[16,4096]{1,0:T(8,128)S(1)} %collective-permute-done.1.refs_1_, f32[16,4096]{1,0:T(8,128)S(1)} %copy-done), custom_call_target="tpu_custom_call" | custom-call | tf_op jit(solution)/shard_map/pallas_call | solution.py:127
  13.8 0.0 collective-permute-done.3.refs_1_
  13.8 0.5 shard_map.92.refs_7_.refs_6_
  14.3 0.0 collective-permute-done.refs_5_
  14.3 0.0 copy-done.2
  14.3 0.0 copy-done.3
  14.3 0.0 copy-done.1
  14.4 0.2 convert_reduce_fusion.2
  14.6 0.4 convert_reduce_fusion
  15.0 0.1 sub.189
  15.1 0.1 fusion.61
  15.2 0.1 fusion.59.refs_0_
  15.3 0.1 select_reduce_fusion.4
  15.4 0.1 fusion.60
  15.5 0.4 select_reduce_fusion.2
  15.9 1.3 %collective-permute-start.4 = (f32[16,4096]{1,0:T(8,128)S(1)}, f32[16,4096]{1,0:T(8,128)S(1)}, u32[]{:S(2)}, u32[]{:S(2)}) collective-permute-start(f32[16,4096]{1,0:T(8,128)S(1)} %collective-permute-done.refs_5_), channel_id=1, source_target_pairs={{0,4},{4,8},{8,12},{12,0},{1,5},{5,9},{9,13},{13,1},{2,6},{6,10},{... | collective-permute-start | bytes 786440 | tf_op jit(solution)/shard_map/ppermute | solution.py:18
  17.2 0.0 collective-permute-done.5.refs_6_
  17.2 4.1 %shard_map.93 = (f32[2112,128]{1,0:T(8,128)S(1)}, bf16[48,128,128]{2,1,0:T(8,128)(2,1)S(1)}) custom-call(s32[4]{0:T(128)S(1)} %select_reduce_fusion.7.refs_0_, s32[4]{0:T(128)S(1)} %and_select_fusion.6.refs_1_, s32[240]{0:T(256)S(1)} %convert_reduce_fusion.5.refs_2_, s32[1920]{0:T(1024)S(1)} %get-tuple-element.44.refs_3_, ...), custom_call_target="tpu_custom_call" | custom-call | tf_op jit(solution)/shard_map/pallas_call | solution.py:315
  21.3 1.4 %select_reduce_fusion = s32[2304]{0:T(1024)S(1)} fusion(s32[1024]{0:T(1024)S(1)} %get-tuple-element.45, s32[1024]{0:T(1024)S(1)} %add_select_fusion.16), kind=kLoop, calls=%fused_computation | loop fusion | flops 7075584 | bytes 17408 | tf_op jit(solution)/shard_map/reduce_sum | solution.py:50
  22.7 1.2 %collective-permute-done.4.refs_5_ = f32[16,4096]{1,0:T(8,128)S(1)} collective-permute-done((f32[16,4096]{1,0:T(8,128)S(1)}, f32[16,4096]{1,0:T(8,128)S(1)}, u32[]{:S(2)}, u32[]{:S(2)}) %collective-permute-start.4) | collective-permute-done | bytes 262176 | tf_op jit(solution)/shard_map/ppermute | solution.py:18
  23.9 2.9 %shard_map.94 = (f32[16,4096]{1,0:T(8,128)S(1)}, f32[16,4096]{1,0:T(8,128)S(1)}, bf16[16,128,128]{2,1,0:T(8,128)(2,1)S(1)}) custom-call(s32[4]{0:T(128)S(1)} %select_reduce_fusion.7.refs_0_, s32[4]{0:T(128)S(1)} %and_select_fusion.6.refs_1_, s32[240]{0:T(256)S(1)} %convert_reduce_fusion.5.refs_2_, s32[1920]{0:T(1024)S(1)} %get-tuple-element.44.refs_3_, ...), custom_call_target="tpu_custom_call" | custom-call | tf_op jit(solution)/shard_map/pallas_call | solution.py:315
  26.8 4.6 %collective-permute-start.6 = (f32[16,4096]{1,0:T(8,128)S(1)}, f32[16,4096]{1,0:T(8,128)S(1)}, u32[]{:S(2)}, u32[]{:S(2)}) collective-permute-start(f32[16,4096]{1,0:T(8,128)S(1)} %get-tuple-element.30), channel_id=1, source_target_pairs={{0,1},{1,0},{2,3},{3,2},{4,5},{5,4},{6,7},{7,6},{8,9},{9,8},{10,11... | collective-permute-start | bytes 786440 | tf_op jit(solution)/shard_map/ppermute | solution.py:18
  31.4 0.1 convert_reduce_fusion.4.refs_2_
  31.6 1.0 %collective-permute-done.6 = f32[16,4096]{1,0:T(8,128)S(1)} collective-permute-done((f32[16,4096]{1,0:T(8,128)S(1)}, f32[16,4096]{1,0:T(8,128)S(1)}, u32[]{:S(2)}, u32[]{:S(2)}) %collective-permute-start.6) | collective-permute-done | bytes 262176 | tf_op jit(solution)/shard_map/ppermute | solution.py:18
  32.6 0.4 collective-permute-start.7
  33.0 0.0 collective-permute-start.8
  33.0 0.2 constant_dynamic-update-slice_fusion.1
  33.2 0.1 constant_dynamic-update-slice_fusion.refs_7_
  33.3 0.9 %collective-permute-done.7.refs_6_ = f32[16,4096]{1,0:T(8,128)S(1)} collective-permute-done((f32[16,4096]{1,0:T(8,128)S(1)}, f32[16,4096]{1,0:T(8,128)S(1)}, u32[]{:S(2)}, u32[]{:S(2)}) %collective-permute-start.7) | collective-permute-done | bytes 262176 | tf_op jit(solution)/shard_map/ppermute | solution.py:18
  34.2 3.7 %shard_map.95.refs_8_ = f32[2112,128]{1,0:T(8,128)S(1)} custom-call(s32[2]{0:T(128)S(1)} %fusion.59.refs_0_, s32[2]{0:T(128)S(1)} %and_select_fusion.2.refs_1_, s32[288]{0:T(512)S(1)} %convert_reduce_fusion.4.refs_2_, s32[2304]{0:T(1024)S(1)} %get-tuple-element.42.refs_3_, s32[2304]{0:T(1024)S(1)} %get-tuple-element.41.refs_4_, ...), custom_call_target="tpu_custom_call" | custom-call | tf_op jit(solution)/shard_map/pallas_call | solution.py:315
  37.9 2.9 %collective-permute-done.8.refs_5_ = f32[16,4096]{1,0:T(8,128)S(1)} collective-permute-done((f32[16,4096]{1,0:T(8,128)S(1)}, f32[16,4096]{1,0:T(8,128)S(1)}, u32[]{:S(2)}, u32[]{:S(2)}) %collective-permute-start.8) | collective-permute-done | bytes 262176 | tf_op jit(solution)/shard_map/ppermute | solution.py:18
  40.8 1.0 %collective-permute-start.9 = (f32[16,4096]{1,0:T(8,128)S(1)}, f32[16,4096]{1,0:T(8,128)S(1)}, u32[]{:S(2)}, u32[]{:S(2)}) collective-permute-start(f32[16,4096]{1,0:T(8,128)S(1)} %collective-permute-done.8.refs_5_), channel_id=1, source_target_pairs={{0,1},{1,0},{2,3},{3,2},{4,5},{5,4},{6,7},{7,6},{8,9},{9,8},{10,11... | collective-permute-start | bytes 786440 | tf_op jit(solution)/shard_map/ppermute | solution.py:18
  41.7 1.2 %collective-permute-done.9.refs_6_ = f32[16,4096]{1,0:T(8,128)S(1)} collective-permute-done((f32[16,4096]{1,0:T(8,128)S(1)}, f32[16,4096]{1,0:T(8,128)S(1)}, u32[]{:S(2)}, u32[]{:S(2)}) %collective-permute-start.9) | collective-permute-done | bytes 262176 | tf_op jit(solution)/shard_map/ppermute | solution.py:18
  42.9 4.3 %shard_map.96 = (f32[16,4096]{1,0:T(8,128)S(1)}, f32[16,4096]{1,0:T(8,128)S(1)}) custom-call(s32[2]{0:T(128)S(1)} %fusion.59.refs_0_, s32[2]{0:T(128)S(1)} %and_select_fusion.2.refs_1_, s32[288]{0:T(512)S(1)} %convert_reduce_fusion.4.refs_2_, s32[2304]{0:T(1024)S(1)} %get-tuple-element.42.refs_3_, s32[2304]{0:T(1024)S(1)} %get-tuple-element.41.refs_4_, ...), custom_call_target="tpu_custom_call" | custom-call | tf_op jit(solution)/shard_map/pallas_call | solution.py:315
  47.2 3.0 %collective-permute-start.10 = (f32[16,4096]{1,0:T(8,128)S(1)}, f32[16,4096]{1,0:T(8,128)S(1)}, u32[]{:S(2)}, u32[]{:S(2)}) collective-permute-start(f32[16,4096]{1,0:T(8,128)S(1)} %get-tuple-element.40), channel_id=1, source_target_pairs={{0,1},{1,0},{2,3},{3,2},{4,5},{5,4},{6,7},{7,6},{8,9},{9,8},{10,11... | collective-permute-start | bytes 786440 | tf_op jit(solution)/shard_map/ppermute | solution.py:18
  50.1 1.2 %collective-permute-done.10 = f32[16,4096]{1,0:T(8,128)S(1)} collective-permute-done((f32[16,4096]{1,0:T(8,128)S(1)}, f32[16,4096]{1,0:T(8,128)S(1)}, u32[]{:S(2)}, u32[]{:S(2)}) %collective-permute-start.10) | collective-permute-done | bytes 262176 | tf_op jit(solution)/shard_map/ppermute | solution.py:18
  51.3 0.7 %multiply_subtract_fusion = f32[16,4096]{1,0:T(8,128)} fusion(f32[16,4096]{1,0:T(8,128)S(1)} %get-tuple-element.39, f32[16,4096]{1,0:T(8,128)S(1)} %collective-permute-done.10, f32[16,4096]{1,0:T(8,128)S(1)} %add.275.refs_5_), kind=kLoop, calls=%fused_computation.12 | loop fusion | flops 262144 | bytes 1048576 | tf_op jit(solution)/shard_map/sub | solution.py:421
  (11 shorter events, 0.2 us)
Async XLA Ops:
  0.0 14.3 %copy-start.2 = (s32[1024]{0:T(1024)S(1)}, s32[1024]{0:T(1024)}, u32[]{:S(2)}) copy-start(s32[1024]{0:T(1024)} %param.14) | copy-start | bytes 12292
  0.0 14.3 %copy-start.3 = (s32[1024]{0:T(1024)S(1)}, s32[1024]{0:T(1024)}, u32[]{:S(2)}) copy-start(s32[1024]{0:T(1024)} %param.15) | copy-start | bytes 12292
  0.0 14.3 %copy-start.1 = (s32[1024]{0:T(1024)S(1)}, s32[1024]{0:T(1024)}, u32[]{:S(2)}) copy-start(s32[1024]{0:T(1024)} %param.16) | copy-start | bytes 12292
  0.0 14.3 %collective-permute-start = (f32[16,4096]{1,0:T(8,128)}, f32[16,4096]{1,0:T(8,128)S(1)}, u32[]{:S(2)}, u32[]{:S(2)}) collective-permute-start(f32[16,4096]{1,0:T(8,128)} %refs_2_.1), channel_id=1, source_target_pairs={{0,4},{4,8},{8,12},{12,0},{1,5},{5,9},{9,13},{13,1},{2,6},{6,10},{... | collective-permute-start | bytes 786440 | tf_op jit(solution)/shard_map/ppermute | solution.py:18
  1.4 10.7 %collective-permute-start.1 = (f32[16,4096]{1,0:T(8,128)}, f32[16,4096]{1,0:T(8,128)S(1)}, u32[]{:S(2)}, u32[]{:S(2)}) collective-permute-start(f32[16,4096]{1,0:T(8,128)} %refs_2_.1), channel_id=1, source_target_pairs={{0,1},{1,0},{2,3},{3,2},{4,5},{5,4},{6,7},{7,6},{8,9},{9,8},{10,11... | collective-permute-start | bytes 786440 | tf_op jit(solution)/shard_map/ppermute | solution.py:18
  2.3 8.1 %collective-permute-start.2 = (f32[16,4096]{1,0:T(8,128)}, f32[16,4096]{1,0:T(8,128)S(1)}, u32[]{:S(2)}, u32[]{:S(2)}) collective-permute-start(f32[16,4096]{1,0:T(8,128)} %refs_2_.1), channel_id=1, source_target_pairs={{0,2},{2,0},{1,3},{3,1},{4,6},{6,4},{5,7},{7,5},{8,10},{10,8},{9,1... | collective-permute-start | bytes 786440 | tf_op jit(solution)/shard_map/ppermute | solution.py:18
  3.5 13.7 %collective-permute-start.5 = (f32[16,4096]{1,0:T(8,128)}, f32[16,4096]{1,0:T(8,128)S(1)}, u32[]{:S(2)}, u32[]{:S(2)}) collective-permute-start(f32[16,4096]{1,0:T(8,128)} %refs_2_.1), channel_id=1, source_target_pairs={{0,12},{4,0},{8,4},{12,8},{1,13},{5,1},{9,5},{13,9},{2,14},{6,2},{... | collective-permute-start | bytes 786440 | tf_op jit(solution)/shard_map/ppermute | solution.py:18
  10.5 3.3 %collective-permute-start.3 = (f32[16,4096]{1,0:T(8,128)S(1)}, f32[16,4096]{1,0:T(8,128)S(1)}, u32[]{:S(2)}, u32[]{:S(2)}) collective-permute-start(f32[16,4096]{1,0:T(8,128)S(1)} %collective-permute-done.2.refs_0_), channel_id=1, source_target_pairs={{0,1},{1,0},{2,3},{3,2},{4,5},{5,4},{6,7},{7,6},{8,9},{9,8},{10,11... | collective-permute-start | bytes 786440 | tf_op jit(solution)/shard_map/ppermute | solution.py:18
  12.0 1.0 %copy-start = (f32[16,4096]{1,0:T(8,128)S(1)}, f32[16,4096]{1,0:T(8,128)}, u32[]{:S(2)}) copy-start(f32[16,4096]{1,0:T(8,128)} %refs_2_.1) | copy-start | bytes 786436
  15.9 8.0 %collective-permute-start.4 = (f32[16,4096]{1,0:T(8,128)S(1)}, f32[16,4096]{1,0:T(8,128)S(1)}, u32[]{:S(2)}, u32[]{:S(2)}) collective-permute-start(f32[16,4096]{1,0:T(8,128)S(1)} %collective-permute-done.refs_5_), channel_id=1, source_target_pairs={{0,4},{4,8},{8,12},{12,0},{1,5},{5,9},{9,13},{13,1},{2,6},{6,10},{... | collective-permute-start | bytes 786440 | tf_op jit(solution)/shard_map/ppermute | solution.py:18
  26.8 5.7 %collective-permute-start.6 = (f32[16,4096]{1,0:T(8,128)S(1)}, f32[16,4096]{1,0:T(8,128)S(1)}, u32[]{:S(2)}, u32[]{:S(2)}) collective-permute-start(f32[16,4096]{1,0:T(8,128)S(1)} %get-tuple-element.30), channel_id=1, source_target_pairs={{0,1},{1,0},{2,3},{3,2},{4,5},{5,4},{6,7},{7,6},{8,9},{9,8},{10,11... | collective-permute-start | bytes 786440 | tf_op jit(solution)/shard_map/ppermute | solution.py:18
  32.6 1.6 %collective-permute-start.7 = (f32[16,4096]{1,0:T(8,128)S(1)}, f32[16,4096]{1,0:T(8,128)S(1)}, u32[]{:S(2)}, u32[]{:S(2)}) collective-permute-start(f32[16,4096]{1,0:T(8,128)S(1)} %add.275.refs_5_), channel_id=1, source_target_pairs={{0,1},{1,0},{2,3},{3,2},{4,5},{5,4},{6,7},{7,6},{8,9},{9,8},{10,11... | collective-permute-start | bytes 786440 | tf_op jit(solution)/shard_map/ppermute | solution.py:18
  33.0 7.8 %collective-permute-start.8 = (f32[16,4096]{1,0:T(8,128)S(1)}, f32[16,4096]{1,0:T(8,128)S(1)}, u32[]{:S(2)}, u32[]{:S(2)}) collective-permute-start(f32[16,4096]{1,0:T(8,128)S(1)} %add.275.refs_5_), channel_id=1, source_target_pairs={{0,2},{2,0},{1,3},{3,1},{4,6},{6,4},{5,7},{7,5},{8,10},{10,8},{9,1... | collective-permute-start | bytes 786440 | tf_op jit(solution)/shard_map/ppermute | solution.py:18
  40.8 2.1 %collective-permute-start.9 = (f32[16,4096]{1,0:T(8,128)S(1)}, f32[16,4096]{1,0:T(8,128)S(1)}, u32[]{:S(2)}, u32[]{:S(2)}) collective-permute-start(f32[16,4096]{1,0:T(8,128)S(1)} %collective-permute-done.8.refs_5_), channel_id=1, source_target_pairs={{0,1},{1,0},{2,3},{3,2},{4,5},{5,4},{6,7},{7,6},{8,9},{9,8},{10,11... | collective-permute-start | bytes 786440 | tf_op jit(solution)/shard_map/ppermute | solution.py:18
  47.2 4.1 %collective-permute-start.10 = (f32[16,4096]{1,0:T(8,128)S(1)}, f32[16,4096]{1,0:T(8,128)S(1)}, u32[]{:S(2)}, u32[]{:S(2)}) collective-permute-start(f32[16,4096]{1,0:T(8,128)S(1)} %get-tuple-element.40), channel_id=1, source_target_pairs={{0,1},{1,0},{2,3},{3,2},{4,5},{5,4},{6,7},{7,6},{8,9},{9,8},{10,11... | collective-permute-start | bytes 786440 | tf_op jit(solution)/shard_map/ppermute | solution.py:18
